TPU v7x, 32 devices: a whole 2x2x4 slice. The times are simulated.
32 devices in a mesh: row: 8 (over y, x, core), tensor: 4 (over z).
Axes of the slice: x: 2, y: 2, z: 4, core: 2. Of those that a mesh axis runs over, the one named last changes fastest.
Arguments:
- latents: bfloat16 [4, 16, 64, 2240], P(None, 'row', None, 'tensor'), may hold values from -6 to 6
- clip_height: int32 [4], replicated, may hold values from 8 to 16, as said below
- clip_width: int32 [4], replicated, may hold values from 32 to 64, as said below
- expand_weight: bfloat16 [2, 2240, 5600], P(None, None, 'tensor'), may hold values from -0.125 to 0.125
- expand_bias: float32 [2, 5600], P(None, 'tensor'), may hold values from -3 to 3
- depth_weight: float32 [3, 3, 2, 5600], P(None, None, None, 'tensor'), may hold values from -2 to 2
- depth_bias: float32 [2, 5600], P(None, 'tensor'), may hold values from -3 to 3
- project_weight: bfloat16 [5600, 2240], P('tensor'), may hold values from -0.109375 to 0.109375
Outputs:
- block_output: bfloat16 [4, 16, 64, 2240], P(None, 'row', None, 'tensor')
Inputs may be any that keep to these rules, and one draw needn't show every extreme that they name: `clip_height`: one clip spans all 16 rows and another exactly 8 of them. `clip_width`: one clip spans all 64 columns and another exactly 32 of them.
All inputs are finite; a program needn't handle non-finite values.
Results may differ from a plain program's by a relative error of at most 0.0062.
Values may be sent and summed in bfloat16 or wider, within the bound.
No kernel may reach another device: no remote copies, remote signals or barrier semaphores. Data moves between devices by JAX's collectives and lax.ppermute only.
A program may use at most 128 MiB of HBM per device.

v0:
```python
import functools

import jax
import jax.numpy as jnp
from jax import lax
from jax.experimental import pallas as pl
from jax.experimental.pallas import tpu as pltpu
from jax.sharding import PartitionSpec as P

LANES = 512
GROUP = 16
TILE = 256


def halo_rows(cells):
    count = lax.axis_size("row")
    ends = count - 1
    head = cells[:, :1]
    tail = cells[:, -1:]
    above = lax.ppermute(tail, "row", [(i, i + 1) for i in range(ends)])
    below = lax.ppermute(head, "row", [(i + 1, i) for i in range(ends)])
    return jnp.concatenate([above, cells, below], axis=1)


def depthwise(padded, depth_weight, depth_bias, row_count, col_count):
    widened = jnp.pad(padded, ((0, 0), (0, 0), (1, 1), (0, 0), (0, 0)))
    out_shape = (widened.shape[0], row_count, col_count) + widened.shape[3:]
    depth_out = jnp.zeros(out_shape, jnp.float32) + depth_bias
    for tap_row in range(3):
        for tap_col in range(3):
            depth_out = (
                depth_out
                + depth_weight[tap_row, tap_col]
                * widened[:, tap_row : tap_row + row_count, tap_col : tap_col + col_count]
            )
    return depth_out


def on_device_plain(
    latents,
    clip_height,
    clip_width,
    expand_weight,
    expand_bias,
    depth_weight,
    depth_bias,
    project_weight,
):
    batch_size, row_count, col_count, depth = latents.shape
    tokens = batch_size * row_count * col_count
    first_row = lax.axis_index("row") * row_count
    row_ids = first_row + jnp.arange(row_count, dtype=jnp.int32)
    col_ids = jnp.arange(col_count, dtype=jnp.int32)
    valid_mask = (
        (row_ids[None, :, None] < clip_height[:, None, None])
        & (col_ids[None, None, :] < clip_width[:, None, None])
    ).astype(jnp.float32)[..., None]
    channels = latents.reshape(tokens, depth).T
    gathered = lax.all_gather(channels, "tensor", axis=0, tiled=True)
    pre_act = jnp.einsum("dt,kdf->tkf", gathered, expand_weight, preferred_element_type=jnp.float32)
    pre_act = pre_act.reshape(batch_size, row_count, col_count, 2, -1)
    expanded = (jax.nn.silu(pre_act + expand_bias) * valid_mask[..., None]).astype(jnp.bfloat16)
    padded = halo_rows(expanded)
    depth_out = depthwise(padded, depth_weight, depth_bias, row_count, col_count)
    hidden = (depth_out[:, :, :, 0] * jax.nn.silu(depth_out[:, :, :, 1])).astype(jnp.bfloat16)
    partial_term = jnp.einsum(
        "tf,fd->dt", hidden.reshape(tokens, -1), project_weight, preferred_element_type=jnp.float32
    ).astype(jnp.bfloat16)
    summed = lax.psum_scatter(partial_term, "tensor", scatter_dimension=0, tiled=True)
    summed = summed.T.reshape(latents.shape).astype(jnp.float32)
    return (summed * valid_mask).astype(jnp.bfloat16)


def slot_clips(width_ref, batch_size):
    narrow, least = jnp.int32(0), width_ref[0]
    for b in range(1, batch_size):
        closer = width_ref[b] < least
        narrow = jnp.where(closer, b, narrow)
        least = jnp.where(closer, width_ref[b], least)
    return [jnp.where(narrow <= s, s + 1, s) for s in range(batch_size - 1)] + [narrow]


def slot_widths(batch_size, col_count):
    return [col_count] * (batch_size - 1) + [col_count // 2]


class Chunk:
    def __init__(self, slots, widths, depth):
        self.slots = slots
        self.widths = [widths[s] for s in slots]
        self.starts = [sum(self.widths[:i]) for i in range(len(slots))]
        self.kept = sum(self.widths)
        self.block = -(-self.kept // 128) * 128
        self.depth, self.rest = depth, depth - LANES
        across = LANES // self.block
        groups = self.rest // GROUP
        self.places = [(g // across * GROUP, g % across * self.block) for g in range(groups)]
        self.lines = self.kept + -(-groups // across) * GROUP
        self.tokens = 2 * self.kept
        self.full, self.left = self.tokens // 128, self.tokens % 128
        self.upper = -(-depth // (2 * GROUP)) * GROUP
        self.unit = (self.full * depth + (self.upper if self.left else 0), 128)

    def clips(self, width_ref, batch_size):
        order = slot_clips(width_ref, batch_size)
        return [order[s] for s in self.slots]

    def mask_column(self, height_ref, width_ref, row_id):
        pieces = []
        clips = self.clips(width_ref, width_ref.shape[0])
        for clip, width in zip(clips, self.widths):
            bound = jnp.where((row_id >= 0) & (row_id < height_ref[clip]), width_ref[clip], 0)
            col = lax.broadcasted_iota(jnp.int32, (width, 128), 0)
            pieces.append((col < bound).astype(jnp.float32))
        return jnp.concatenate(pieces, axis=0)

    def put_unit(self, unit_ref, sums):
        depth, at = self.depth, self.full * self.depth
        for b in range(self.full):
            unit_ref[b * depth : (b + 1) * depth, :] = sums[:, b * 128 : (b + 1) * 128]
        if self.left:
            tail = sums[:, self.full * 128 :]
            lower = depth - self.upper
            unit_ref[at : at + self.upper, : self.left] = tail[: self.upper]
            unit_ref[at : at + lower, self.left :] = tail[self.upper :]
            if lower < self.upper:
                unit_ref[at + lower :, self.left :] = jnp.zeros(
                    (self.upper - lower, 128 - self.left), sums.dtype
                )

    def get_unit(self, unit):
        depth, at = self.depth, self.full * self.depth
        blocks = [unit[b * depth : (b + 1) * depth, :] for b in range(self.full)]
        if self.left:
            lower = depth - self.upper
            blocks.append(
                jnp.concatenate(
                    [unit[at : at + self.upper, : self.left], unit[at : at + lower, self.left :]], axis=0
                )
            )
        return jnp.concatenate(blocks, axis=1)


def parity_of():
    return lax.rem(lax.axis_index("row"), 2)


def row_of(place, parity):
    return jnp.where(parity == 0, (-1, 0, 1, 2)[place], (2, 1, 0, -1)[place])


def silu(v):
    h = 0.5 * v
    return h + h * jnp.tanh(h)


def pack_kernel(width_ref, x_ref, *out_refs, chunks):
    parity = parity_of()
    for chunk, out_ref in zip(chunks, out_refs):
        for place in range(2):
            row = jnp.where(parity == 0, 1 - place, place)
            tails = []
            for clip, width, at in zip(
                chunk.clips(width_ref, x_ref.shape[0]), chunk.widths, chunk.starts
            ):
                out_ref[place, at : at + width, :] = x_ref[clip, row, :width, :LANES]
                tails.append(x_ref[clip, row, :width, LANES:].astype(jnp.float32))
            if chunk.block > chunk.kept:
                tails.append(jnp.zeros((chunk.block - chunk.kept, chunk.rest), jnp.float32))
            turned = jnp.concatenate(tails, axis=0).T.astype(jnp.bfloat16)
            kept = chunk.kept
            out_ref[place, kept:, :] = jnp.zeros((chunk.lines - kept, LANES), jnp.bfloat16)
            for g, (down, over) in enumerate(chunk.places):
                out_ref[place, kept + down : kept + down + GROUP, over : over + chunk.block] = turned[
                    g * GROUP : (g + 1) * GROUP
                ]


def tiles_of(hidden_count):
    return [slice(at, min(at + TILE, hidden_count)) for at in range(0, hidden_count, TILE)]


def gather_rows(x_scr, chunk, rows):
    kept = chunk.kept
    for place, packets in enumerate(rows):
        lines = slice(place * kept, (place + 1) * kept)
        tails = []
        for j, packet in enumerate(packets):
            x_scr[lines, j * LANES : (j + 1) * LANES] = packet[:kept, :]
            for down, over in chunk.places:
                tails.append(packet[kept + down : kept + down + GROUP, over : over + chunk.block])
        turned = jnp.concatenate(tails, axis=0).astype(jnp.float32).T
        x_scr[lines, len(packets) * LANES :] = turned[:kept].astype(jnp.bfloat16)


def load_kernel(w_ref, out_ref, token_ref, sems, *, shards, depth):
    token_ref[...] = jnp.zeros_like(token_ref)
    me = lax.axis_index("tensor")
    rest = depth - LANES
    copies = []
    for k in range(2):
        for j in range(shards):
            base = lax.bitwise_xor(me, j) * depth
            for part, (source, size, target) in enumerate(
                ((base, LANES, j * LANES), (base + LANES, rest, shards * LANES + j * rest))
            ):
                copies.append(
                    pltpu.make_async_copy(
                        w_ref.at[k, pl.ds(pl.multiple_of(source, GROUP), size)],
                        out_ref.at[k, pl.ds(target, size)],
                        sems.at[k, j, part],
                    )
                )
    for copy in copies:
        copy.start()
    for copy in copies:
        copy.wait()


def table_kernel(height_ref, width_ref, dw_ref, eb_ref, db_ref, par_ref, *mask_refs, chunks):
    parity = parity_of()
    for chunk, mask_ref in zip(chunks, mask_refs):
        for place in range(4):
            row_id = lax.axis_index("row") * 2 + row_of(place, parity)
            mask_ref[place] = chunk.mask_column(height_ref, width_ref, row_id)
    for i in range(3):
        for col in range(3):
            par_ref[i * 6 + col * 2 : i * 6 + col * 2 + 2, :] = dw_ref[i, col]
    par_ref[18:20, :] = eb_ref[...]
    par_ref[20:22, :] = db_ref[...]


def expand(x_scr, w_ref, par_ref, k, units):
    pre_act = jnp.dot(x_scr[...], w_ref[k, :, units], preferred_element_type=jnp.float32)
    return silu(pre_act + par_ref[18 + k : 19 + k, units])


def masked(cells, mask):
    width = cells.shape[1]
    return cells * jnp.concatenate([mask] * -(-width // 128), axis=1)[:, :width]


def own_kernel(*refs, chunk, shards):
    packet_refs, (mask_ref, par_ref, w_ref, out_ref, x_scr) = refs[:shards], refs[shards:]
    kept = chunk.kept
    gather_rows(x_scr, chunk, [[p.at[1] for p in packet_refs], [p.at[0] for p in packet_refs]])
    mask = jnp.concatenate([mask_ref[1], mask_ref[2]], axis=0)
    for units in tiles_of(w_ref.shape[2]):
        for k in range(2):
            out_ref[k, :, units] = masked(expand(x_scr, w_ref, par_ref, k, units), mask)


def hidden_kernel(*refs, chunk, shards, groups):
    count = len(groups)
    inner_refs, outer_refs = refs[:count], refs[count : 2 * count]
    own_ref, mask_ref, par_ref, w_ref, out_ref, x_scr = refs[2 * count :]
    kept = chunk.kept
    parity = parity_of()
    spots = {j: (g, i) for g, js in enumerate(groups) for i, j in enumerate(js)}
    gather_rows(
        x_scr,
        chunk,
        [[refs_of[spots[j][0]].at[spots[j][1]] for j in range(shards)] for refs_of in (outer_refs, inner_refs)],
    )
    mask = jnp.concatenate([mask_ref[0], mask_ref[3]], axis=0)

    def around(units):
        return [
            masked(expand(x_scr, w_ref, par_ref, k, units), mask) for k in range(2)
        ]

    def convolve(units, cells):
        width = units.stop - units.start
        line = lax.broadcasted_iota(jnp.int32, (kept, width), 0)
        not_first, not_last = None, None
        for at, size in zip(chunk.starts, chunk.widths):
            first, last = line != at, line != at + size - 1
            not_first = first if not_first is None else not_first & first
            not_last = last if not_last is None else not_last & last
        halves = ([], [])
        for k in range(2):
            rows = [
                cells[k][:kept],
                own_ref[k, :kept, units],
                own_ref[k, kept:, units],
                cells[k][kept:],
            ]
            taps = [
                [
                    jnp.where(
                        parity == 0,
                        par_ref[i * 6 + col * 2 + k : i * 6 + col * 2 + k + 1, units],
                        par_ref[(2 - i) * 6 + col * 2 + k : (2 - i) * 6 + col * 2 + k + 1, units],
                    )
                    for col in range(3)
                ]
                for i in range(3)
            ]
            for place in range(2):
                sums = []
                for tap_col in range(3):
                    total = None
                    for i in range(3):
                        term = taps[i][tap_col] * rows[place + i]
                        total = term if total is None else total + term
                    sums.append(total)
                left = jnp.where(not_first, pltpu.roll(sums[0], 1, 0), 0.0)
                right = jnp.where(not_last, pltpu.roll(sums[2], kept - 1, 0), 0.0)
                halves[k].append(sums[1] + left + right + par_ref[20 + k : 21 + k, units])
        for place in range(2):
            hidden = halves[0][place] * silu(halves[1][place])
            out_ref[(1 - place) * kept : (2 - place) * kept, units] = hidden.astype(jnp.bfloat16)

    tiles = tiles_of(w_ref.shape[2])
    cells = around(tiles[0])
    for t, units in enumerate(tiles):
        coming = around(tiles[t + 1]) if t + 1 < len(tiles) else None
        convolve(units, cells)
        cells = coming


def project(weight_ref, hidden_ref, depth, j):
    start = lax.bitwise_xor(lax.axis_index("tensor"), j) * depth
    return lax.dot_general(
        weight_ref[pl.ds(pl.multiple_of(start, GROUP), depth), :],
        hidden_ref[...],
        (((1,), (1,)), ((), ())),
        preferred_element_type=jnp.float32,
    )


def unit_kernel(weight_ref, hidden_ref, *refs, chunk, j):
    out_ref = refs[-1]
    sums = project(weight_ref, hidden_ref, chunk.depth, j)
    for ref in refs[:-1]:
        sums = sums + chunk.get_unit(ref[...].astype(jnp.float32))
    chunk.put_unit(out_ref, sums.astype(jnp.bfloat16))


def share_kernel(weight_ref, hidden_ref, unit_ref, out_ref, *, chunk):
    sums = project(weight_ref, hidden_ref, chunk.depth, 0)
    out_ref[...] = sums + chunk.get_unit(unit_ref[...].astype(jnp.float32))


def final_kernel(width_ref, mask_ref, share_ref, *refs, chunk, sources):
    out_ref = refs[-1]
    if len(refs) > sources + 1:
        out_ref[...] = refs[sources][...]
    sums = share_ref[...]
    for ref in refs[:sources]:
        sums = sums + chunk.get_unit(ref[...].astype(jnp.float32))
    cells = sums.T
    parity = parity_of()
    for place in range(2):
        row = jnp.where(parity == 0, 1 - place, place)
        mask = mask_ref[2 - place][:, :1] > 0
        part = cells[place * chunk.kept : (place + 1) * chunk.kept]
        part = jnp.where(mask, part, 0.0).astype(jnp.bfloat16)
        clips = chunk.clips(width_ref, width_ref.shape[0])
        for clip, width, at in zip(clips, chunk.widths, chunk.starts):
            out_ref[clip, row, :width, :] = part[at : at + width]
            if width < out_ref.shape[2]:
                blank = jnp.zeros((out_ref.shape[2] - width, chunk.depth), jnp.bfloat16)
                out_ref[clip, row, width:, :] = blank


VMEM = pl.BlockSpec(memory_space=pltpu.VMEM)
MIB = 1024 * 1024


def after(value, *others):
    return lax.optimization_barrier((value,) + others)[0]


def on_device_packed(
    latents,
    clip_height,
    clip_width,
    expand_weight,
    expand_bias,
    depth_weight,
    depth_bias,
    project_weight,
):
    batch_size, row_count, col_count, depth = latents.shape
    shards, row_devices = lax.axis_size("tensor"), lax.axis_size("row")
    hidden_count = expand_weight.shape[2]
    full_depth = shards * depth
    chunks = chunks_of(batch_size, col_count, depth)
    count = len(chunks)
    own = pl.pallas_call(
        functools.partial(pack_kernel, chunks=chunks),
        out_shape=[jax.ShapeDtypeStruct((2, c.lines, LANES), jnp.bfloat16) for c in chunks],
        grid_spec=pltpu.PrefetchScalarGridSpec(
            num_scalar_prefetch=1, grid=(), in_specs=[VMEM], out_specs=[VMEM] * count
        ),
        compiler_params=pltpu.CompilerParams(vmem_limit_bytes=16 * MIB),
        name="pack",
    )(clip_width, latents)
    project_turned = project_weight.T

    sibling = [(i, i ^ 1) for i in range(row_devices)]
    beyond = [(i, i + 1) for i in range(1, row_devices - 1, 2)]
    beyond = beyond + [(b, a) for a, b in beyond]
    near = [(i, i ^ 1) for i in range(4)]
    two_off = [(i, i ^ 2) for i in range(4)]
    opposite = [(i, i ^ 3) for i in range(4)]
    middle = [(1, 2), (2, 1)]
    to_end = [(2, 3), (1, 0)]
    from_end = [(0, 1), (3, 2)]

    def edge_rows(packets, groups):
        return [
            [jnp.concatenate([packets[j][side : side + 1] for j in js], axis=0) for js in groups]
            for side in range(2)
        ]

    def send_rows(inner, outer):
        return (
            [lax.ppermute(x, "row", sibling) for x in inner],
            [lax.ppermute(x, "row", beyond) for x in outer],
        )

    def relay(mine, tables, *others):
        second = lax.ppermute(mine, "tensor", two_off)
        first = lax.ppermute(mine, "tensor", near)
        across = lax.ppermute(after(mine, second, *others), "tensor", middle)
        passed = lax.ppermute(after(second, *others), "tensor", to_end)
        return [mine, first, second, after(across, tables) + passed]

    def direct(mine):
        third, second, first = [
            lax.ppermute(mine, "tensor", pairs) for pairs in (opposite, two_off, near)
        ]
        return [mine, first, second, third]

    out = None
    weights, token = pl.pallas_call(
        functools.partial(load_kernel, shards=shards, depth=depth),
        out_shape=[
            jax.ShapeDtypeStruct(expand_weight.shape, jnp.bfloat16),
            jax.ShapeDtypeStruct((8, 128), jnp.float32),
        ],
        in_specs=[pl.BlockSpec(memory_space=pl.ANY)],
        out_specs=[VMEM, VMEM],
        scratch_shapes=[pltpu.SemaphoreType.DMA((2, shards, 2))],
        compiler_params=pltpu.CompilerParams(vmem_limit_bytes=36 * MIB),
        name="load_weights",
    )(after(expand_weight, own[0]))
    taps = after(depth_weight, token)
    parameters, *masks = pl.pallas_call(
        functools.partial(table_kernel, chunks=chunks),
        out_shape=[jax.ShapeDtypeStruct((22, hidden_count), jnp.float32)]
        + [jax.ShapeDtypeStruct((4, c.kept, 128), jnp.float32) for c in chunks],
        grid_spec=pltpu.PrefetchScalarGridSpec(
            num_scalar_prefetch=2, grid=(), in_specs=[VMEM] * 3, out_specs=[VMEM] * (1 + count)
        ),
        compiler_params=pltpu.CompilerParams(vmem_limit_bytes=16 * MIB),
        name="tables",
    )(clip_height, clip_width, taps, expand_bias, depth_bias)
    groups = ((0,), (1, 2), (3,))
    inner, outer = send_rows(*edge_rows(own[:1], groups[:1]))
    packets = relay(own[0], parameters, token, *inner, *outer)
    edges = edge_rows(packets, groups[1:])
    later = send_rows(*edges)
    inner, outer = inner + later[0], outer + later[1]
    upcoming = direct(after(own[1], edges[0][-1], edges[1][-1]))
    for number, chunk in enumerate(chunks):
        if number:
            packets, groups = list(lax.optimization_barrier((*upcoming, hidden))[:shards]), ((0, 1, 2, 3),)
            inner, outer = send_rows(*edge_rows(packets, groups))
            packets[0] = after(packets[0], far)
        rows = pl.pallas_call(
            functools.partial(own_kernel, chunk=chunk, shards=shards),
            out_shape=jax.ShapeDtypeStruct((2, chunk.tokens, hidden_count), jnp.float32),
            in_specs=[VMEM] * (shards + 3),
            out_specs=VMEM,
            scratch_shapes=[pltpu.VMEM((chunk.tokens, full_depth), jnp.bfloat16)],
            compiler_params=pltpu.CompilerParams(vmem_limit_bytes=16 * MIB),
            cost_estimate=pl.CostEstimate(
                flops=1000,
                bytes_accessed=1000,
                transcendentals=0,
            ),
            name="expand_own",
        )(*packets, masks[number], parameters, weights)
        if number:
            inner[0] = after(inner[0], last_unit)
        hidden = pl.pallas_call(
            functools.partial(hidden_kernel, chunk=chunk, shards=shards, groups=groups),
            out_shape=jax.ShapeDtypeStruct((chunk.tokens, hidden_count), jnp.bfloat16),
            in_specs=[VMEM] * (2 * len(groups) + 4),
            out_specs=VMEM,
            scratch_shapes=[pltpu.VMEM((chunk.tokens, full_depth), jnp.bfloat16)],
            compiler_params=pltpu.CompilerParams(vmem_limit_bytes=16 * MIB),
            cost_estimate=pl.CostEstimate(
                flops=1000,
                bytes_accessed=1000,
                transcendentals=0,
            ),
            name="expand_conv",
        )(*inner, *outer, rows, masks[number], parameters, weights)

        cost = pl.CostEstimate(
            flops=2 * chunk.tokens * depth * hidden_count,
            bytes_accessed=2 * depth * hidden_count + 2 * chunk.tokens * hidden_count,
            transcendentals=0,
        )

        def unit(j, *added):
            return pl.pallas_call(
                functools.partial(unit_kernel, chunk=chunk, j=j),
                out_shape=jax.ShapeDtypeStruct(chunk.unit, jnp.bfloat16),
                in_specs=[VMEM] * (2 + len(added)),
                out_specs=VMEM,
                compiler_params=pltpu.CompilerParams(vmem_limit_bytes=16 * MIB),
                cost_estimate=cost,
                name=f"project_{j}",
            )(project_turned, hidden, *added)

        far = unit(3)
        relayed = lax.ppermute(far, "tensor", from_end)
        across = lax.ppermute(far, "tensor", middle)
        close = unit(1)
        if number:
            relayed, across = lax.optimization_barrier((relayed, across, out))[:2]
        else:
            relayed, across = lax.optimization_barrier((relayed, across))
        last_unit = unit(2, relayed)
        distant = lax.ppermute(last_unit, "tensor", two_off)
        arrived = [across, lax.ppermute(after(close, last_unit), "tensor", near)]
        share = pl.pallas_call(
            functools.partial(share_kernel, chunk=chunk),
            out_shape=jax.ShapeDtypeStruct((depth, chunk.tokens), jnp.float32),
            in_specs=[VMEM] * 3,
            out_specs=VMEM,
            compiler_params=pltpu.CompilerParams(vmem_limit_bytes=16 * MIB),
            cost_estimate=pl.CostEstimate(flops=10**10, bytes_accessed=10**8, transcendentals=0),
            name="project_0",
        )(project_turned, hidden, distant)
        extra = [] if out is None else [out]
        out = pl.pallas_call(
            functools.partial(final_kernel, chunk=chunk, sources=len(arrived)),
            out_shape=jax.ShapeDtypeStruct(latents.shape, jnp.bfloat16),
            grid_spec=pltpu.PrefetchScalarGridSpec(
                num_scalar_prefetch=1,
                grid=(),
                in_specs=[VMEM] * (2 + len(arrived) + len(extra)),
                out_specs=VMEM,
            ),
            compiler_params=pltpu.CompilerParams(vmem_limit_bytes=16 * MIB),
            cost_estimate=pl.CostEstimate(flops=10**11, bytes_accessed=10**9, transcendentals=0),
            name="finish",
        )(clip_width, masks[number], share, *arrived, *extra)
    return out


def chunks_of(batch_size, col_count, depth):
    widths = slot_widths(batch_size, col_count)
    half = batch_size // 2
    return [Chunk(slots, widths, depth) for slots in (list(range(half)), list(range(half, batch_size)))]


def on_device(latents, clip_height, clip_width, expand_weight, *rest_of):
    batch_size, row_count, col_count, depth = latents.shape
    fits = (
        batch_size >= 2
        and row_count == 2
        and lax.axis_size("row") % 2 == 0
        and lax.axis_size("tensor") == 4
        and depth > LANES
        and (depth - LANES) % GROUP == 0
        and depth % GROUP == 0
        and all(
            c.block in (128, 256, 512) and c.kept % GROUP == 0 and c.left in (0, 64)
            for c in chunks_of(batch_size, col_count, depth)
        )
    )
    run = on_device_packed if fits else on_device_plain
    return run(latents, clip_height, clip_width, expand_weight, *rest_of)


def solution(mesh):
    in_specs = (
        P(None, "row", None, "tensor"),
        P(),
        P(),
        P(None, None, "tensor"),
        P(None, "tensor"),
        P(None, None, None, "tensor"),
        P(None, "tensor"),
        P("tensor", None),
    )
    out_specs = P(None, "row", None, "tensor")
    return jax.shard_map(
        on_device, mesh=mesh, in_specs=in_specs, out_specs=out_specs, check_vma=False
    )
```

profile of v0, /device:TPU:2, one launch (start us, length us, event | category | flops | bytes accessed | tf_op | source)
XLA Modules:
  0.0 99.3 jit_solution(4693299500329495624)
XLA Ops:
  0.0 1.1 %copy-done = bf16[4,2,64,560]{3,2,1,0:T(8,128)(2,1)S(1)} copy-done((bf16[4,2,64,560]{3,2,1,0:T(8,128)(2,1)S(1)}, bf16[4,2,64,560]{3,2,1,0:T(8,128)(2,1)}, u32[]{:S(2)}) %copy-start) | copy-done | bytes 573464
  1.1 0.7 copy-done.4
  1.7 0.7 pack.1
  2.4 2.7 %collective-permute-start = (bf16[2,144,512]{2,1,0:T(8,128)(2,1)S(1)}, bf16[2,144,512]{2,1,0:T(8,128)(2,1)S(1)}, u32[]{:S(2)}, u32[]{:S(2)}) collective-permute-start(bf16[2,144,512]{2,1,0:T(8,128)(2,1)S(1)} %get-tuple-element.36.refs_0_), channel_id=1, source_target_pairs={{0,2},{1,3},{2,0},{3,1},{4,6},{5,7},{6,4},{7,5},{8,10},{9,11},{10,... | collective-permute-start | bytes 884744 | tf_op jit(solution)/shard_map/ppermute | solution.py:425
  5.1 0.1 collective-permute-start.1
  5.2 2.6 %collective-permute-start.2 = (bf16[1,144,512]{2,1,0:T(8,128)(2,1)S(1)}, bf16[1,144,512]{2,1,0:T(8,128)(2,1)S(1)}, u32[]{:S(2)}, u32[]{:S(2)}) collective-permute-start(bf16[1,144,512]{2,1,0:T(8,128)(2,1)S(1)} %get-tuple-element.61), channel_id=1, source_target_pairs={{4,8},{12,16},{20,24},{8,4},{16,12},{24,20},{5,9},{13,17},{21,25},... | collective-permute-start | bytes 442376 | tf_op jit(solution)/shard_map/ppermute | solution.py:421
  7.9 1.6 %collective-permute-start.8 = (bf16[2,144,512]{2,1,0:T(8,128)(2,1)S(1)}, bf16[2,144,512]{2,1,0:T(8,128)(2,1)S(1)}, u32[]{:S(2)}, u32[]{:S(2)}) collective-permute-start(bf16[2,144,512]{2,1,0:T(8,128)(2,1)S(1)} %get-tuple-element.36.refs_0_), channel_id=1, source_target_pairs={{0,1},{1,0},{2,3},{3,2},{4,5},{5,4},{6,7},{7,6},{8,9},{9,8},{10,11... | collective-permute-start | bytes 884744 | tf_op jit(solution)/shard_map/ppermute | solution.py:426
  9.5 5.3 %load_weights.1 = (bf16[2,2240,1400]{2,1,0:T(8,128)(2,1)S(1)}, f32[8,128]{1,0:T(8,128)}) custom-call(bf16[2,2240,1400]{2,1,0:T(8,128)(2,1)} %w_ref), custom_call_target="tpu_custom_call" | custom-call | tf_op jit(solution)/shard_map/load_weights/pallas_call | solution.py:438
  14.9 3.7 %collective-permute-done.refs_2_ = bf16[2,144,512]{2,1,0:T(8,128)(2,1)S(1)} collective-permute-done((bf16[2,144,512]{2,1,0:T(8,128)(2,1)S(1)}, bf16[2,144,512]{2,1,0:T(8,128)(2,1)S(1)}, u32[]{:S(2)}, u32[]{:S(2)}) %collective-permute-start) | collective-permute-done | bytes 294944 | tf_op jit(solution)/shard_map/ppermute | solution.py:425
  18.5 0.7 collective-permute-start.3
  19.2 1.3 %collective-permute-start.4 = (bf16[2,144,512]{2,1,0:T(8,128)(2,1)S(1)}, bf16[2,144,512]{2,1,0:T(8,128)(2,1)S(1)}, u32[]{:S(2)}, u32[]{:S(2)}) collective-permute-start(bf16[2,144,512]{2,1,0:T(8,128)(2,1)S(1)} %collective-permute-done.refs_2_), channel_id=1, source_target_pairs={{2,3},{1,0},{6,7},{5,4},{10,11},{9,8},{14,15},{13,12},{18,19},{17,... | collective-permute-start | bytes 884744 | tf_op jit(solution)/shard_map/ppermute | solution.py:428
  20.5 2.4 %collective-permute-done.8.refs_1_ = bf16[2,144,512]{2,1,0:T(8,128)(2,1)S(1)} collective-permute-done((bf16[2,144,512]{2,1,0:T(8,128)(2,1)S(1)}, bf16[2,144,512]{2,1,0:T(8,128)(2,1)S(1)}, u32[]{:S(2)}, u32[]{:S(2)}) %collective-permute-start.8) | collective-permute-done | bytes 294944 | tf_op jit(solution)/shard_map/ppermute | solution.py:426
  23.0 1.9 %collective-permute-start.11 = (bf16[2,144,512]{2,1,0:T(8,128)(2,1)S(1)}, bf16[2,144,512]{2,1,0:T(8,128)(2,1)S(1)}, u32[]{:S(2)}, u32[]{:S(2)}) collective-permute-start(bf16[2,144,512]{2,1,0:T(8,128)(2,1)S(1)} %pad_maximum_fusion.3), channel_id=1, source_target_pairs={{4,8},{12,16},{20,24},{8,4},{16,12},{24,20},{5,9},{13,17},{21,25},... | collective-permute-start | bytes 884744 | tf_op jit(solution)/shard_map/ppermute | solution.py:421
  25.0 1.7 %collective-permute-start.9 = (bf16[2,144,512]{2,1,0:T(8,128)(2,1)S(1)}, bf16[2,144,512]{2,1,0:T(8,128)(2,1)S(1)}, u32[]{:S(2)}, u32[]{:S(2)}) collective-permute-start(bf16[2,144,512]{2,1,0:T(8,128)(2,1)S(1)} %pad_maximum_fusion.2), channel_id=1, source_target_pairs={{0,4},{4,0},{8,12},{12,8},{16,20},{20,16},{24,28},{28,24},{1,5},{5... | collective-permute-start | bytes 884744 | tf_op jit(solution)/shard_map/ppermute | solution.py:420
  26.7 0.6 tables.1
  27.4 2.1 %collective-permute-done.4 = bf16[2,144,512]{2,1,0:T(8,128)(2,1)S(1)} collective-permute-done((bf16[2,144,512]{2,1,0:T(8,128)(2,1)S(1)}, bf16[2,144,512]{2,1,0:T(8,128)(2,1)S(1)}, u32[]{:S(2)}, u32[]{:S(2)}) %collective-permute-start.4) | collective-permute-done | bytes 294944 | tf_op jit(solution)/shard_map/ppermute | solution.py:428
  29.5 0.1 add.3.refs_3_
  29.6 0.5 collective-permute-start.5
  30.1 4.1 %collective-permute-start.6 = (bf16[2,112,512]{2,1,0:T(8,128)(2,1)S(1)}, bf16[2,112,512]{2,1,0:T(8,128)(2,1)S(1)}, u32[]{:S(2)}, u32[]{:S(2)}) collective-permute-start(bf16[2,112,512]{2,1,0:T(8,128)(2,1)S(1)} %get-tuple-element.49.refs_0_), channel_id=1, source_target_pairs={{0,2},{1,3},{2,0},{3,1},{4,6},{5,7},{6,4},{7,5},{8,10},{9,11},{10,... | collective-permute-start | bytes 688136 | tf_op jit(solution)/shard_map/ppermute | solution.py:433
  34.2 2.5 %collective-permute-start.12 = (bf16[1,144,512]{2,1,0:T(8,128)(2,1)S(1)}, bf16[1,144,512]{2,1,0:T(8,128)(2,1)S(1)}, u32[]{:S(2)}, u32[]{:S(2)}) collective-permute-start(bf16[1,144,512]{2,1,0:T(8,128)(2,1)S(1)} %get-tuple-element.59), channel_id=1, source_target_pairs={{4,8},{12,16},{20,24},{8,4},{16,12},{24,20},{5,9},{13,17},{21,25},... | collective-permute-start | bytes 442376 | tf_op jit(solution)/shard_map/ppermute | solution.py:421
  36.8 4.0 %expand_own.2.refs_6_ = f32[2,256,1400]{2,1,0:T(8,128)S(1)} custom-call(bf16[2,144,512]{2,1,0:T(8,128)(2,1)S(1)} %get-tuple-element.36.refs_0_, bf16[2,144,512]{2,1,0:T(8,128)(2,1)S(1)} %collective-permute-done.8.refs_1_, bf16[2,144,512]{2,1,0:T(8,128)(2,1)S(1)} %collective-permute-done.refs_2_, bf16[2,144,512]{2,1,0:T(8,128)(2,1)S(1)} %add.3.refs_3_, ...), custom_call_target="tpu_custom_call" | custom-call | flops 1000 | bytes 1000 | tf_op jit(solution)/shard_map/expand_own/pallas_call | solution.py:473
  40.8 6.8 %expand_conv.2.hidden_ref = bf16[256,1400]{1,0:T(8,128)(2,1)S(1)} custom-call(bf16[1,144,512]{2,1,0:T(8,128)(2,1)S(1)} %collective-permute-done.1.refs_0_, bf16[2,144,512]{2,1,0:T(8,128)(2,1)S(1)} %collective-permute-done.9.refs_1_, bf16[1,144,512]{2,1,0:T(8,128)(2,1)S(1)} %collective-permute-done.10.refs_2_, ...), custom_call_target="tpu_custom_call" | custom-call | flops 1000 | bytes 1000 | tf_op jit(solution)/shard_map/expand_conv/pallas_call | solution.py:489
  47.7 0.6 project_3.2
  48.3 2.5 %collective-permute-start.14 = (bf16[1120,128]{1,0:T(8,128)(2,1)S(1)}, bf16[1120,128]{1,0:T(8,128)(2,1)S(1)}, u32[]{:S(2)}, u32[]{:S(2)}) collective-permute-start(bf16[1120,128]{1,0:T(8,128)(2,1)S(1)} %project_3.2), channel_id=1, source_target_pairs={{0,1},{3,2},{4,5},{7,6},{8,9},{11,10},{12,13},{15,14},{16,17},{19,... | collective-permute-start | bytes 860168 | tf_op jit(solution)/shard_map/ppermute | solution.py:522
  50.8 0.7 collective-permute-start.15
  51.6 0.1 pad_maximum_fusion
  51.7 2.3 %collective-permute-start.13 = (bf16[4,112,512]{2,1,0:T(8,128)(2,1)S(1)}, bf16[4,112,512]{2,1,0:T(8,128)(2,1)S(1)}, u32[]{:S(2)}, u32[]{:S(2)}) collective-permute-start(bf16[4,112,512]{2,1,0:T(8,128)(2,1)S(1)} %pad_maximum_fusion), channel_id=1, source_target_pairs={{0,4},{4,0},{8,12},{12,8},{16,20},{20,16},{24,28},{28,24},{1,5},{5... | collective-permute-start | bytes 1376264 | tf_op jit(solution)/shard_map/ppermute | solution.py:420
  54.1 2.1 %collective-permute-start.16 = (bf16[4,112,512]{2,1,0:T(8,128)(2,1)S(1)}, bf16[4,112,512]{2,1,0:T(8,128)(2,1)S(1)}, u32[]{:S(2)}, u32[]{:S(2)}) collective-permute-start(bf16[4,112,512]{2,1,0:T(8,128)(2,1)S(1)} %pad_maximum_fusion.1), channel_id=1, source_target_pairs={{4,8},{12,16},{20,24},{8,4},{16,12},{24,20},{5,9},{13,17},{21,25},... | collective-permute-start | bytes 1376264 | tf_op jit(solution)/shard_map/ppermute | solution.py:421
  56.2 0.3 collective-permute-done.14.refs_0_
  56.4 0.6 project_2.2
  57.1 6.6 %collective-permute-start.19 = (bf16[1120,128]{1,0:T(8,128)(2,1)S(1)}, bf16[1120,128]{1,0:T(8,128)(2,1)S(1)}, u32[]{:S(2)}, u32[]{:S(2)}) collective-permute-start(bf16[1120,128]{1,0:T(8,128)(2,1)S(1)} %project_2.2), channel_id=1, source_target_pairs={{0,2},{1,3},{2,0},{3,1},{4,6},{5,7},{6,4},{7,5},{8,10},{9,11},{10,... | collective-permute-start | bytes 860168 | tf_op jit(solution)/shard_map/ppermute | solution.py:530
  63.7 0.6 project_1.2
  64.3 3.1 %expand_own.3.refs_2_ = f32[2,192,1400]{2,1,0:T(8,128)S(1)} custom-call(bf16[2,112,512]{2,1,0:T(8,128)(2,1)S(1)} %get-tuple-element.49.refs_0_, bf16[2,112,512]{2,1,0:T(8,128)(2,1)S(1)} %collective-permute-done.5.refs_1_, bf16[2,112,512]{2,1,0:T(8,128)(2,1)S(1)} %collective-permute-done.6.refs_2_, bf16[2,112,512]{2,1,0:T(8,128)(2,1)S(1)} %collective-permute-done.7.refs_3_, ...), custom_call_target="tpu_custom_call" | custom-call | flops 1000 | bytes 1000 | tf_op jit(solution)/shard_map/expand_own/pallas_call | solution.py:473
  67.4 0.1 collective-permute-start.20
  67.5 5.2 %expand_conv.3.hidden_ref = bf16[192,1400]{1,0:T(8,128)(2,1)S(1)} custom-call(bf16[4,112,512]{2,1,0:T(8,128)(2,1)S(1)} %collective-permute-done.13.refs_0_, bf16[4,112,512]{2,1,0:T(8,128)(2,1)S(1)} %collective-permute-done.16.refs_1_, f32[2,192,1400]{2,1,0:T(8,128)S(1)} %expand_own.3.refs_2_, f32[4,96,128]{2,1,0:T(8,128)S(1)} %get-tuple-element.34.refs_4_.refs_3_.mask_ref, ...), custom_call_target="tpu_custom_call" | custom-call | flops 1000 | bytes 1000 | tf_op jit(solution)/shard_map/expand_conv/pallas_call | solution.py:489
  72.6 0.7 project_3.3
  73.3 3.9 %collective-permute-start.17 = (bf16[848,128]{1,0:T(8,128)(2,1)S(1)}, bf16[848,128]{1,0:T(8,128)(2,1)S(1)}, u32[]{:S(2)}, u32[]{:S(2)}) collective-permute-start(bf16[848,128]{1,0:T(8,128)(2,1)S(1)} %project_3.3), channel_id=1, source_target_pairs={{0,1},{3,2},{4,5},{7,6},{8,9},{11,10},{12,13},{15,14},{16,17},{19,... | collective-permute-start | bytes 651272 | tf_op jit(solution)/shard_map/ppermute | solution.py:522
  77.3 0.7 collective-permute-start.18
  78.0 0.7 project_0.2.share_ref
  78.6 3.6 %collective-permute-done.20.refs_1_ = bf16[1120,128]{1,0:T(8,128)(2,1)S(1)} collective-permute-done((bf16[1120,128]{1,0:T(8,128)(2,1)S(1)}, bf16[1120,128]{1,0:T(8,128)(2,1)S(1)}, u32[]{:S(2)}, u32[]{:S(2)}) %collective-permute-start.20) | collective-permute-done | bytes 286752 | tf_op jit(solution)/shard_map/ppermute | solution.py:531
  82.3 0.8 finish.2.refs_2_
  83.1 0.7 project_2.3
  83.8 2.0 %collective-permute-start.21 = (bf16[848,128]{1,0:T(8,128)(2,1)S(1)}, bf16[848,128]{1,0:T(8,128)(2,1)S(1)}, u32[]{:S(2)}, u32[]{:S(2)}) collective-permute-start(bf16[848,128]{1,0:T(8,128)(2,1)S(1)} %project_2.3), channel_id=1, source_target_pairs={{0,2},{1,3},{2,0},{3,1},{4,6},{5,7},{6,4},{7,5},{8,10},{9,11},{10,... | collective-permute-start | bytes 651272 | tf_op jit(solution)/shard_map/ppermute | solution.py:530
  85.8 0.7 project_1.3
  86.5 1.1 %collective-permute-start.22 = (bf16[848,128]{1,0:T(8,128)(2,1)S(1)}, bf16[848,128]{1,0:T(8,128)(2,1)S(1)}, u32[]{:S(2)}, u32[]{:S(2)}) collective-permute-start(bf16[848,128]{1,0:T(8,128)(2,1)S(1)} %project_1.3), channel_id=1, source_target_pairs={{0,1},{1,0},{2,3},{3,2},{4,5},{5,4},{6,7},{7,6},{8,9},{9,8},{10,11... | collective-permute-start | bytes 651272 | tf_op jit(solution)/shard_map/ppermute | solution.py:531
  87.6 9.4 %collective-permute-done.21.unit_ref = bf16[848,128]{1,0:T(8,128)(2,1)S(1)} collective-permute-done((bf16[848,128]{1,0:T(8,128)(2,1)S(1)}, bf16[848,128]{1,0:T(8,128)(2,1)S(1)}, u32[]{:S(2)}, u32[]{:S(2)}) %collective-permute-start.21) | collective-permute-done | bytes 217120 | tf_op jit(solution)/shard_map/ppermute | solution.py:530
  96.9 0.6 project_0.3.share_ref
  97.6 1.7 %finish.3 = bf16[4,2,64,560]{3,2,1,0:T(8,128)(2,1)} custom-call(s32[4]{0:T(128)S(1)} %copy-done.5, f32[4,96,128]{2,1,0:T(8,128)S(1)} %get-tuple-element.34.refs_4_.refs_3_.mask_ref, f32[560,192]{1,0:T(8,128)S(1)} %project_0.3.share_ref, bf16[848,128]{1,0:T(8,128)(2,1)S(1)} %collective-permute-done.18.refs_0_, ...), custom_call_target="tpu_custom_call" | custom-call | flops 99999997952 | bytes 1000000000 | tf_op jit(solution)/shard_map/finish/pallas_call | solution.py:542
  (45 shorter events, 0.4 us)
Async XLA Ops:
  0.0 1.1 %copy-start = (bf16[4,2,64,560]{3,2,1,0:T(8,128)(2,1)S(1)}, bf16[4,2,64,560]{3,2,1,0:T(8,128)(2,1)}, u32[]{:S(2)}) copy-start(bf16[4,2,64,560]{3,2,1,0:T(8,128)(2,1)} %x_ref.1) | copy-start | bytes 1720324
  1.1 0.7 copy-start.4
  2.4 16.1 %collective-permute-start = (bf16[2,144,512]{2,1,0:T(8,128)(2,1)S(1)}, bf16[2,144,512]{2,1,0:T(8,128)(2,1)S(1)}, u32[]{:S(2)}, u32[]{:S(2)}) collective-permute-start(bf16[2,144,512]{2,1,0:T(8,128)(2,1)S(1)} %get-tuple-element.36.refs_0_), channel_id=1, source_target_pairs={{0,2},{1,3},{2,0},{3,1},{4,6},{5,7},{6,4},{7,5},{8,10},{9,11},{10,... | collective-permute-start | bytes 884744 | tf_op jit(solution)/shard_map/ppermute | solution.py:425
  5.1 9.8 %collective-permute-start.1 = (bf16[1,144,512]{2,1,0:T(8,128)(2,1)S(1)}, bf16[1,144,512]{2,1,0:T(8,128)(2,1)S(1)}, u32[]{:S(2)}, u32[]{:S(2)}) collective-permute-start(bf16[1,144,512]{2,1,0:T(8,128)(2,1)S(1)} %get-tuple-element.62), channel_id=1, source_target_pairs={{0,4},{4,0},{8,12},{12,8},{16,20},{20,16},{24,28},{28,24},{1,5},{5... | collective-permute-start | bytes 442376 | tf_op jit(solution)/shard_map/ppermute | solution.py:420
  5.2 21.6 %copy-start.1 = (f32[3,3,2,1400]{3,2,1,0:T(2,128)S(1)}, f32[3,3,2,1400]{3,2,1,0:T(2,128)}, u32[]{:S(2)}) copy-start(f32[3,3,2,1400]{3,2,1,0:T(2,128)} %dw_ref) | copy-start | bytes 302404
  5.2 21.6 %copy-start.2 = (f32[2,1400]{1,0:T(2,128)S(1)}, f32[2,1400]{1,0:T(2,128)}, u32[]{:S(2)}) copy-start(f32[2,1400]{1,0:T(2,128)} %eb_ref.1) | copy-start | bytes 33604
  5.2 21.6 %copy-start.3 = (f32[2,1400]{1,0:T(2,128)S(1)}, f32[2,1400]{1,0:T(2,128)}, u32[]{:S(2)}) copy-start(f32[2,1400]{1,0:T(2,128)} %db_ref.1) | copy-start | bytes 33604
  5.2 21.6 %copy-start.6 = (s32[4]{0:T(128)S(1)}, s32[4]{0:T(128)}, u32[]{:S(2)}) copy-start(s32[4]{0:T(128)} %height_ref.1) | copy-start | bytes 52
  5.2 9.6 %collective-permute-start.2 = (bf16[1,144,512]{2,1,0:T(8,128)(2,1)S(1)}, bf16[1,144,512]{2,1,0:T(8,128)(2,1)S(1)}, u32[]{:S(2)}, u32[]{:S(2)}) collective-permute-start(bf16[1,144,512]{2,1,0:T(8,128)(2,1)S(1)} %get-tuple-element.61), channel_id=1, source_target_pairs={{4,8},{12,16},{20,24},{8,4},{16,12},{24,20},{5,9},{13,17},{21,25},... | collective-permute-start | bytes 442376 | tf_op jit(solution)/shard_map/ppermute | solution.py:421
  7.9 15.1 %collective-permute-start.8 = (bf16[2,144,512]{2,1,0:T(8,128)(2,1)S(1)}, bf16[2,144,512]{2,1,0:T(8,128)(2,1)S(1)}, u32[]{:S(2)}, u32[]{:S(2)}) collective-permute-start(bf16[2,144,512]{2,1,0:T(8,128)(2,1)S(1)} %get-tuple-element.36.refs_0_), channel_id=1, source_target_pairs={{0,1},{1,0},{2,3},{3,2},{4,5},{5,4},{6,7},{7,6},{8,9},{9,8},{10,11... | collective-permute-start | bytes 884744 | tf_op jit(solution)/shard_map/ppermute | solution.py:426
  18.5 8.8 %collective-permute-start.3 = (bf16[2,144,512]{2,1,0:T(8,128)(2,1)S(1)}, bf16[2,144,512]{2,1,0:T(8,128)(2,1)S(1)}, u32[]{:S(2)}, u32[]{:S(2)}) collective-permute-start(bf16[2,144,512]{2,1,0:T(8,128)(2,1)S(1)} %get-tuple-element.36.refs_0_), channel_id=1, source_target_pairs={{1,2},{2,1},{5,6},{6,5},{9,10},{10,9},{13,14},{14,13},{17,18},{18,... | collective-permute-start | bytes 884744 | tf_op jit(solution)/shard_map/ppermute | solution.py:427
  19.2 10.3 %collective-permute-start.4 = (bf16[2,144,512]{2,1,0:T(8,128)(2,1)S(1)}, bf16[2,144,512]{2,1,0:T(8,128)(2,1)S(1)}, u32[]{:S(2)}, u32[]{:S(2)}) collective-permute-start(bf16[2,144,512]{2,1,0:T(8,128)(2,1)S(1)} %collective-permute-done.refs_2_), channel_id=1, source_target_pairs={{2,3},{1,0},{6,7},{5,4},{10,11},{9,8},{14,15},{13,12},{18,19},{17,... | collective-permute-start | bytes 884744 | tf_op jit(solution)/shard_map/ppermute | solution.py:428
  23.0 11.2 %collective-permute-start.11 = (bf16[2,144,512]{2,1,0:T(8,128)(2,1)S(1)}, bf16[2,144,512]{2,1,0:T(8,128)(2,1)S(1)}, u32[]{:S(2)}, u32[]{:S(2)}) collective-permute-start(bf16[2,144,512]{2,1,0:T(8,128)(2,1)S(1)} %pad_maximum_fusion.3), channel_id=1, source_target_pairs={{4,8},{12,16},{20,24},{8,4},{16,12},{24,20},{5,9},{13,17},{21,25},... | collective-permute-start | bytes 884744 | tf_op jit(solution)/shard_map/ppermute | solution.py:421
  25.0 9.2 %collective-permute-start.9 = (bf16[2,144,512]{2,1,0:T(8,128)(2,1)S(1)}, bf16[2,144,512]{2,1,0:T(8,128)(2,1)S(1)}, u32[]{:S(2)}, u32[]{:S(2)}) collective-permute-start(bf16[2,144,512]{2,1,0:T(8,128)(2,1)S(1)} %pad_maximum_fusion.2), channel_id=1, source_target_pairs={{0,4},{4,0},{8,12},{12,8},{16,20},{20,16},{24,28},{28,24},{1,5},{5... | collective-permute-start | bytes 884744 | tf_op jit(solution)/shard_map/ppermute | solution.py:420
  29.6 21.9 %collective-permute-start.5 = (bf16[2,112,512]{2,1,0:T(8,128)(2,1)S(1)}, bf16[2,112,512]{2,1,0:T(8,128)(2,1)S(1)}, u32[]{:S(2)}, u32[]{:S(2)}) collective-permute-start(bf16[2,112,512]{2,1,0:T(8,128)(2,1)S(1)} %get-tuple-element.49.refs_0_), channel_id=1, source_target_pairs={{0,1},{1,0},{2,3},{3,2},{4,5},{5,4},{6,7},{7,6},{8,9},{9,8},{10,11... | collective-permute-start | bytes 688136 | tf_op jit(solution)/shard_map/ppermute | solution.py:433
  30.1 21.4 %collective-permute-start.6 = (bf16[2,112,512]{2,1,0:T(8,128)(2,1)S(1)}, bf16[2,112,512]{2,1,0:T(8,128)(2,1)S(1)}, u32[]{:S(2)}, u32[]{:S(2)}) collective-permute-start(bf16[2,112,512]{2,1,0:T(8,128)(2,1)S(1)} %get-tuple-element.49.refs_0_), channel_id=1, source_target_pairs={{0,2},{1,3},{2,0},{3,1},{4,6},{5,7},{6,4},{7,5},{8,10},{9,11},{10,... | collective-permute-start | bytes 688136 | tf_op jit(solution)/shard_map/ppermute | solution.py:433
  34.2 17.3 %collective-permute-start.7 = (bf16[2,112,512]{2,1,0:T(8,128)(2,1)S(1)}, bf16[2,112,512]{2,1,0:T(8,128)(2,1)S(1)}, u32[]{:S(2)}, u32[]{:S(2)}) collective-permute-start(bf16[2,112,512]{2,1,0:T(8,128)(2,1)S(1)} %get-tuple-element.49.refs_0_), channel_id=1, source_target_pairs={{0,3},{1,2},{2,1},{3,0},{4,7},{5,6},{6,5},{7,4},{8,11},{9,10},{10,... | collective-permute-start | bytes 688136 | tf_op jit(solution)/shard_map/ppermute | solution.py:433
  34.2 6.6 %collective-permute-start.10 = (bf16[1,144,512]{2,1,0:T(8,128)(2,1)S(1)}, bf16[1,144,512]{2,1,0:T(8,128)(2,1)S(1)}, u32[]{:S(2)}, u32[]{:S(2)}) collective-permute-start(bf16[1,144,512]{2,1,0:T(8,128)(2,1)S(1)} %get-tuple-element.60), channel_id=1, source_target_pairs={{0,4},{4,0},{8,12},{12,8},{16,20},{20,16},{24,28},{28,24},{1,5},{5... | collective-permute-start | bytes 442376 | tf_op jit(solution)/shard_map/ppermute | solution.py:420
  34.2 6.6 %collective-permute-start.12 = (bf16[1,144,512]{2,1,0:T(8,128)(2,1)S(1)}, bf16[1,144,512]{2,1,0:T(8,128)(2,1)S(1)}, u32[]{:S(2)}, u32[]{:S(2)}) collective-permute-start(bf16[1,144,512]{2,1,0:T(8,128)(2,1)S(1)} %get-tuple-element.59), channel_id=1, source_target_pairs={{4,8},{12,16},{20,24},{8,4},{16,12},{24,20},{5,9},{13,17},{21,25},... | collective-permute-start | bytes 442376 | tf_op jit(solution)/shard_map/ppermute | solution.py:421
  36.8 10.9 %slice-start = ((s8[6307840]{0:T(1024)(128)(4,1)}), s8[4194304]{0:T(1024)(128)(4,1)S(1)}, s32[]{:S(2)}) async-start(s8[6307840]{0:T(1024)(128)(4,1)} %bitcast.1), calls=%async_computation | async-start | bytes 8388608
  40.8 6.9 %slice-start.1 = ((s8[6307840]{0:T(1024)(128)(4,1)}), s8[2113536]{0:T(1024)(128)(4,1)S(1)}, s32[]{:S(2)}) async-start(s8[6307840]{0:T(1024)(128)(4,1)} %bitcast.1), calls=%async_computation.1 | async-start | bytes 4227072
  48.3 8.1 %collective-permute-start.14 = (bf16[1120,128]{1,0:T(8,128)(2,1)S(1)}, bf16[1120,128]{1,0:T(8,128)(2,1)S(1)}, u32[]{:S(2)}, u32[]{:S(2)}) collective-permute-start(bf16[1120,128]{1,0:T(8,128)(2,1)S(1)} %project_3.2), channel_id=1, source_target_pairs={{0,1},{3,2},{4,5},{7,6},{8,9},{11,10},{12,13},{15,14},{16,17},{19,... | collective-permute-start | bytes 860168 | tf_op jit(solution)/shard_map/ppermute | solution.py:522
  50.8 5.6 %collective-permute-start.15 = (bf16[1120,128]{1,0:T(8,128)(2,1)S(1)}, bf16[1120,128]{1,0:T(8,128)(2,1)S(1)}, u32[]{:S(2)}, u32[]{:S(2)}) collective-permute-start(bf16[1120,128]{1,0:T(8,128)(2,1)S(1)} %project_3.2), channel_id=1, source_target_pairs={{1,2},{2,1},{5,6},{6,5},{9,10},{10,9},{13,14},{14,13},{17,18},{18,... | collective-permute-start | bytes 860168 | tf_op jit(solution)/shard_map/ppermute | solution.py:523
  51.7 15.8 %collective-permute-start.13 = (bf16[4,112,512]{2,1,0:T(8,128)(2,1)S(1)}, bf16[4,112,512]{2,1,0:T(8,128)(2,1)S(1)}, u32[]{:S(2)}, u32[]{:S(2)}) collective-permute-start(bf16[4,112,512]{2,1,0:T(8,128)(2,1)S(1)} %pad_maximum_fusion), channel_id=1, source_target_pairs={{0,4},{4,0},{8,12},{12,8},{16,20},{20,16},{24,28},{28,24},{1,5},{5... | collective-permute-start | bytes 1376264 | tf_op jit(solution)/shard_map/ppermute | solution.py:420
  54.1 13.4 %collective-permute-start.16 = (bf16[4,112,512]{2,1,0:T(8,128)(2,1)S(1)}, bf16[4,112,512]{2,1,0:T(8,128)(2,1)S(1)}, u32[]{:S(2)}, u32[]{:S(2)}) collective-permute-start(bf16[4,112,512]{2,1,0:T(8,128)(2,1)S(1)} %pad_maximum_fusion.1), channel_id=1, source_target_pairs={{4,8},{12,16},{20,24},{8,4},{16,12},{24,20},{5,9},{13,17},{21,25},... | collective-permute-start | bytes 1376264 | tf_op jit(solution)/shard_map/ppermute | solution.py:421
  57.1 20.9 %collective-permute-start.19 = (bf16[1120,128]{1,0:T(8,128)(2,1)S(1)}, bf16[1120,128]{1,0:T(8,128)(2,1)S(1)}, u32[]{:S(2)}, u32[]{:S(2)}) collective-permute-start(bf16[1120,128]{1,0:T(8,128)(2,1)S(1)} %project_2.2), channel_id=1, source_target_pairs={{0,2},{1,3},{2,0},{3,1},{4,6},{5,7},{6,4},{7,5},{8,10},{9,11},{10,... | collective-permute-start | bytes 860168 | tf_op jit(solution)/shard_map/ppermute | solution.py:530
  67.4 14.9 %collective-permute-start.20 = (bf16[1120,128]{1,0:T(8,128)(2,1)S(1)}, bf16[1120,128]{1,0:T(8,128)(2,1)S(1)}, u32[]{:S(2)}, u32[]{:S(2)}) collective-permute-start(bf16[1120,128]{1,0:T(8,128)(2,1)S(1)} %project_1.2), channel_id=1, source_target_pairs={{0,1},{1,0},{2,3},{3,2},{4,5},{5,4},{6,7},{7,6},{8,9},{9,8},{10,11... | collective-permute-start | bytes 860168 | tf_op jit(solution)/shard_map/ppermute | solution.py:531
  73.3 8.9 %copy-start.5 = (s32[4]{0:T(128)S(1)}, s32[4]{0:T(128)}, u32[]{:S(2)}) copy-start(s32[4]{0:T(128)} %width_ref.7) | copy-start | bytes 52
  73.3 9.7 %collective-permute-start.17 = (bf16[848,128]{1,0:T(8,128)(2,1)S(1)}, bf16[848,128]{1,0:T(8,128)(2,1)S(1)}, u32[]{:S(2)}, u32[]{:S(2)}) collective-permute-start(bf16[848,128]{1,0:T(8,128)(2,1)S(1)} %project_3.3), channel_id=1, source_target_pairs={{0,1},{3,2},{4,5},{7,6},{8,9},{11,10},{12,13},{15,14},{16,17},{19,... | collective-permute-start | bytes 651272 | tf_op jit(solution)/shard_map/ppermute | solution.py:522
  77.3 5.8 %collective-permute-start.18 = (bf16[848,128]{1,0:T(8,128)(2,1)S(1)}, bf16[848,128]{1,0:T(8,128)(2,1)S(1)}, u32[]{:S(2)}, u32[]{:S(2)}) collective-permute-start(bf16[848,128]{1,0:T(8,128)(2,1)S(1)} %project_3.3), channel_id=1, source_target_pairs={{1,2},{2,1},{5,6},{6,5},{9,10},{10,9},{13,14},{14,13},{17,18},{18,... | collective-permute-start | bytes 651272 | tf_op jit(solution)/shard_map/ppermute | solution.py:523
  83.8 13.2 %collective-permute-start.21 = (bf16[848,128]{1,0:T(8,128)(2,1)S(1)}, bf16[848,128]{1,0:T(8,128)(2,1)S(1)}, u32[]{:S(2)}, u32[]{:S(2)}) collective-permute-start(bf16[848,128]{1,0:T(8,128)(2,1)S(1)} %project_2.3), channel_id=1, source_target_pairs={{0,2},{1,3},{2,0},{3,1},{4,6},{5,7},{6,4},{7,5},{8,10},{9,11},{10,... | collective-permute-start | bytes 651272 | tf_op jit(solution)/shard_map/ppermute | solution.py:530
  86.5 11.1 %collective-permute-start.22 = (bf16[848,128]{1,0:T(8,128)(2,1)S(1)}, bf16[848,128]{1,0:T(8,128)(2,1)S(1)}, u32[]{:S(2)}, u32[]{:S(2)}) collective-permute-start(bf16[848,128]{1,0:T(8,128)(2,1)S(1)} %project_1.3), channel_id=1, source_target_pairs={{0,1},{1,0},{2,3},{3,2},{4,5},{5,4},{6,7},{7,6},{8,9},{9,8},{10,11... | collective-permute-start | bytes 651272 | tf_op jit(solution)/shard_map/ppermute | solution.py:531
where the time goes:
time: 99.8 us; the launch traced here: 99.3 us
  starting transfers between devices  41.6 us (42%)
  Pallas kernels  33.4 us (33%)
  waiting for transfers between devices  21.6 us (22%)
  local copies, waits for them, and re-layouts  1.94 us (2%)
    pallas_call x2, Pallas kernels, on_device_packed(): pl.pallas_call(functools.partial(hidden_kernel, chunk=chunk, shards=shard...  12 us
    ppermute x2, waiting for transfers between devices, on_device_packed(): distant = lax.ppermute(last_unit, 'tensor', two_off)  9.38 us
    ppermute x4, starting transfers between devices, send_rows(): lax.ppermute(x, 'row', beyond)  9.19 us
    ppermute x2, starting transfers between devices, on_device_packed(): distant = lax.ppermute(last_unit, 'tensor', two_off)  8.57 us
    pallas_call x2, Pallas kernels, on_device_packed(): pl.pallas_call(functools.partial(own_kernel, chunk=chunk, shards=shards),...  7.06 us
    ppermute x2, starting transfers between devices, on_device_packed(): relayed = lax.ppermute(far, 'tensor', from_end)  6.41 us
    pallas_call x1, Pallas kernels, on_device_packed(): pl.pallas_call(functools.partial(load_kernel, shards=shards, depth=depth)...  5.33 us
    ppermute x3, starting transfers between devices, direct(): lax.ppermute(mine, 'tensor', pairs)  4.57 us
  transfers between devices with their start and end apart: 23, of which 6 were waited for; matrix products, arithmetic and copies ran while one was open for 0% of the time, Pallas kernels for 31%

commit v1 on v0

--- a/solution.py
+++ b/solution.py
@@ -523,12 +523,13 @@
         across = lax.ppermute(far, "tensor", middle)
         close = unit(1)
         if number:
-            relayed, across = lax.optimization_barrier((relayed, across, out))[:2]
+            relayed = after(relayed, out)
         else:
             relayed, across = lax.optimization_barrier((relayed, across))
         last_unit = unit(2, relayed)
         distant = lax.ppermute(last_unit, "tensor", two_off)
-        arrived = [across, lax.ppermute(after(close, last_unit), "tensor", near)]
+        close = after(close, last_unit, across) if number else after(close, last_unit)
+        arrived = [across, lax.ppermute(close, "tensor", near)]
         share = pl.pallas_call(
             functools.partial(share_kernel, chunk=chunk),
             out_shape=jax.ShapeDtypeStruct((depth, chunk.tokens), jnp.float32),

time: 99.8 us -> 99.4 us (level)
  starting transfers between devices: 41.6 us -> 40.3 us
  waiting for transfers between devices: 21.6 us -> 22.6 us
    ppermute x2, starting transfers between devices: 8.57 us -> 6.65 us  [on_device_packed(): distant = lax.ppermute(last_unit, 'tensor', two_off)]
where the time goes in v1:
time: 99.4 us; the launch traced here: 99 us
  starting transfers between devices  40.3 us (41%)
  Pallas kernels  33.4 us (34%)
  waiting for transfers between devices  22.6 us (23%)
  local copies, waits for them, and re-layouts  1.94 us (2%)
    pallas_call x2, Pallas kernels, on_device_packed(): pl.pallas_call(functools.partial(hidden_kernel, chunk=chunk, shards=shard...  12 us
    ppermute x2, waiting for transfers between devices, on_device_packed(): distant = lax.ppermute(last_unit, 'tensor', two_off)  10.4 us
    ppermute x4, starting transfers between devices, send_rows(): lax.ppermute(x, 'row', beyond)  9.19 us
    pallas_call x2, Pallas kernels, on_device_packed(): pl.pallas_call(functools.partial(own_kernel, chunk=chunk, shards=shards),...  7.06 us
    ppermute x2, starting transfers between devices, on_device_packed(): distant = lax.ppermute(last_unit, 'tensor', two_off)  6.65 us
    ppermute x2, starting transfers between devices, on_device_packed(): relayed = lax.ppermute(far, 'tensor', from_end)  6.41 us
    pallas_call x1, Pallas kernels, on_device_packed(): pl.pallas_call(functools.partial(load_kernel, shards=shards, depth=depth)...  5.33 us
    ppermute x3, starting transfers between devices, direct(): lax.ppermute(mine, 'tensor', pairs)  4.57 us
  transfers between devices with their start and end apart: 23, of which 6 were waited for; matrix products, arithmetic and copies ran while one was open for 0% of the time, Pallas kernels for 31%

profile of v1, /device:TPU:2, one launch (start us, length us, event | category | flops | bytes accessed | tf_op | source)
XLA Modules:
  0.0 99.0 jit_solution(8443299757913192054)
XLA Ops:
  0.0 1.1 %copy-done = bf16[4,2,64,560]{3,2,1,0:T(8,128)(2,1)S(1)} copy-done((bf16[4,2,64,560]{3,2,1,0:T(8,128)(2,1)S(1)}, bf16[4,2,64,560]{3,2,1,0:T(8,128)(2,1)}, u32[]{:S(2)}) %copy-start) | copy-done | bytes 573464
  1.1 0.7 copy-done.4
  1.7 0.7 pack.1
  2.4 2.7 %collective-permute-start = (bf16[2,144,512]{2,1,0:T(8,128)(2,1)S(1)}, bf16[2,144,512]{2,1,0:T(8,128)(2,1)S(1)}, u32[]{:S(2)}, u32[]{:S(2)}) collective-permute-start(bf16[2,144,512]{2,1,0:T(8,128)(2,1)S(1)} %get-tuple-element.35.refs_0_), channel_id=1, source_target_pairs={{0,2},{1,3},{2,0},{3,1},{4,6},{5,7},{6,4},{7,5},{8,10},{9,11},{10,... | collective-permute-start | bytes 884744 | tf_op jit(solution)/shard_map/ppermute | solution.py:425
  5.1 0.1 collective-permute-start.1
  5.2 2.6 %collective-permute-start.2 = (bf16[1,144,512]{2,1,0:T(8,128)(2,1)S(1)}, bf16[1,144,512]{2,1,0:T(8,128)(2,1)S(1)}, u32[]{:S(2)}, u32[]{:S(2)}) collective-permute-start(bf16[1,144,512]{2,1,0:T(8,128)(2,1)S(1)} %get-tuple-element.59), channel_id=1, source_target_pairs={{4,8},{12,16},{20,24},{8,4},{16,12},{24,20},{5,9},{13,17},{21,25},... | collective-permute-start | bytes 442376 | tf_op jit(solution)/shard_map/ppermute | solution.py:421
  7.9 1.6 %collective-permute-start.8 = (bf16[2,144,512]{2,1,0:T(8,128)(2,1)S(1)}, bf16[2,144,512]{2,1,0:T(8,128)(2,1)S(1)}, u32[]{:S(2)}, u32[]{:S(2)}) collective-permute-start(bf16[2,144,512]{2,1,0:T(8,128)(2,1)S(1)} %get-tuple-element.35.refs_0_), channel_id=1, source_target_pairs={{0,1},{1,0},{2,3},{3,2},{4,5},{5,4},{6,7},{7,6},{8,9},{9,8},{10,11... | collective-permute-start | bytes 884744 | tf_op jit(solution)/shard_map/ppermute | solution.py:426
  9.5 5.3 %load_weights.1 = (bf16[2,2240,1400]{2,1,0:T(8,128)(2,1)S(1)}, f32[8,128]{1,0:T(8,128)}) custom-call(bf16[2,2240,1400]{2,1,0:T(8,128)(2,1)} %w_ref), custom_call_target="tpu_custom_call" | custom-call | tf_op jit(solution)/shard_map/load_weights/pallas_call | solution.py:438
  14.9 3.7 %collective-permute-done.refs_2_ = bf16[2,144,512]{2,1,0:T(8,128)(2,1)S(1)} collective-permute-done((bf16[2,144,512]{2,1,0:T(8,128)(2,1)S(1)}, bf16[2,144,512]{2,1,0:T(8,128)(2,1)S(1)}, u32[]{:S(2)}, u32[]{:S(2)}) %collective-permute-start) | collective-permute-done | bytes 294944 | tf_op jit(solution)/shard_map/ppermute | solution.py:425
  18.5 0.7 collective-permute-start.3
  19.2 1.3 %collective-permute-start.4 = (bf16[2,144,512]{2,1,0:T(8,128)(2,1)S(1)}, bf16[2,144,512]{2,1,0:T(8,128)(2,1)S(1)}, u32[]{:S(2)}, u32[]{:S(2)}) collective-permute-start(bf16[2,144,512]{2,1,0:T(8,128)(2,1)S(1)} %collective-permute-done.refs_2_), channel_id=1, source_target_pairs={{2,3},{1,0},{6,7},{5,4},{10,11},{9,8},{14,15},{13,12},{18,19},{17,... | collective-permute-start | bytes 884744 | tf_op jit(solution)/shard_map/ppermute | solution.py:428
  20.5 2.4 %collective-permute-done.8.refs_1_ = bf16[2,144,512]{2,1,0:T(8,128)(2,1)S(1)} collective-permute-done((bf16[2,144,512]{2,1,0:T(8,128)(2,1)S(1)}, bf16[2,144,512]{2,1,0:T(8,128)(2,1)S(1)}, u32[]{:S(2)}, u32[]{:S(2)}) %collective-permute-start.8) | collective-permute-done | bytes 294944 | tf_op jit(solution)/shard_map/ppermute | solution.py:426
  23.0 1.9 %collective-permute-start.11 = (bf16[2,144,512]{2,1,0:T(8,128)(2,1)S(1)}, bf16[2,144,512]{2,1,0:T(8,128)(2,1)S(1)}, u32[]{:S(2)}, u32[]{:S(2)}) collective-permute-start(bf16[2,144,512]{2,1,0:T(8,128)(2,1)S(1)} %pad_maximum_fusion.3), channel_id=1, source_target_pairs={{4,8},{12,16},{20,24},{8,4},{16,12},{24,20},{5,9},{13,17},{21,25},... | collective-permute-start | bytes 884744 | tf_op jit(solution)/shard_map/ppermute | solution.py:421
  25.0 1.7 %collective-permute-start.9 = (bf16[2,144,512]{2,1,0:T(8,128)(2,1)S(1)}, bf16[2,144,512]{2,1,0:T(8,128)(2,1)S(1)}, u32[]{:S(2)}, u32[]{:S(2)}) collective-permute-start(bf16[2,144,512]{2,1,0:T(8,128)(2,1)S(1)} %pad_maximum_fusion.2), channel_id=1, source_target_pairs={{0,4},{4,0},{8,12},{12,8},{16,20},{20,16},{24,28},{28,24},{1,5},{5... | collective-permute-start | bytes 884744 | tf_op jit(solution)/shard_map/ppermute | solution.py:420
  26.7 0.6 tables.1
  27.4 2.1 %collective-permute-done.4 = bf16[2,144,512]{2,1,0:T(8,128)(2,1)S(1)} collective-permute-done((bf16[2,144,512]{2,1,0:T(8,128)(2,1)S(1)}, bf16[2,144,512]{2,1,0:T(8,128)(2,1)S(1)}, u32[]{:S(2)}, u32[]{:S(2)}) %collective-permute-start.4) | collective-permute-done | bytes 294944 | tf_op jit(solution)/shard_map/ppermute | solution.py:428
  29.5 0.1 add.3.refs_3_
  29.6 0.5 collective-permute-start.5
  30.1 4.1 %collective-permute-start.6 = (bf16[2,112,512]{2,1,0:T(8,128)(2,1)S(1)}, bf16[2,112,512]{2,1,0:T(8,128)(2,1)S(1)}, u32[]{:S(2)}, u32[]{:S(2)}) collective-permute-start(bf16[2,112,512]{2,1,0:T(8,128)(2,1)S(1)} %get-tuple-element.48.refs_0_), channel_id=1, source_target_pairs={{0,2},{1,3},{2,0},{3,1},{4,6},{5,7},{6,4},{7,5},{8,10},{9,11},{10,... | collective-permute-start | bytes 688136 | tf_op jit(solution)/shard_map/ppermute | solution.py:433
  34.2 2.5 %collective-permute-start.12 = (bf16[1,144,512]{2,1,0:T(8,128)(2,1)S(1)}, bf16[1,144,512]{2,1,0:T(8,128)(2,1)S(1)}, u32[]{:S(2)}, u32[]{:S(2)}) collective-permute-start(bf16[1,144,512]{2,1,0:T(8,128)(2,1)S(1)} %get-tuple-element.57), channel_id=1, source_target_pairs={{4,8},{12,16},{20,24},{8,4},{16,12},{24,20},{5,9},{13,17},{21,25},... | collective-permute-start | bytes 442376 | tf_op jit(solution)/shard_map/ppermute | solution.py:421
  36.8 4.0 %expand_own.2.refs_6_ = f32[2,256,1400]{2,1,0:T(8,128)S(1)} custom-call(bf16[2,144,512]{2,1,0:T(8,128)(2,1)S(1)} %get-tuple-element.35.refs_0_, bf16[2,144,512]{2,1,0:T(8,128)(2,1)S(1)} %collective-permute-done.8.refs_1_, bf16[2,144,512]{2,1,0:T(8,128)(2,1)S(1)} %collective-permute-done.refs_2_, bf16[2,144,512]{2,1,0:T(8,128)(2,1)S(1)} %add.3.refs_3_, ...), custom_call_target="tpu_custom_call" | custom-call | flops 1000 | bytes 1000 | tf_op jit(solution)/shard_map/expand_own/pallas_call | solution.py:473
  40.8 6.8 %expand_conv.2.hidden_ref = bf16[256,1400]{1,0:T(8,128)(2,1)S(1)} custom-call(bf16[1,144,512]{2,1,0:T(8,128)(2,1)S(1)} %collective-permute-done.1.refs_0_, bf16[2,144,512]{2,1,0:T(8,128)(2,1)S(1)} %collective-permute-done.9.refs_1_, bf16[1,144,512]{2,1,0:T(8,128)(2,1)S(1)} %collective-permute-done.10.refs_2_, ...), custom_call_target="tpu_custom_call" | custom-call | flops 1000 | bytes 1000 | tf_op jit(solution)/shard_map/expand_conv/pallas_call | solution.py:489
  47.7 0.6 project_3.2
  48.3 2.5 %collective-permute-start.14 = (bf16[1120,128]{1,0:T(8,128)(2,1)S(1)}, bf16[1120,128]{1,0:T(8,128)(2,1)S(1)}, u32[]{:S(2)}, u32[]{:S(2)}) collective-permute-start(bf16[1120,128]{1,0:T(8,128)(2,1)S(1)} %project_3.2), channel_id=1, source_target_pairs={{0,1},{3,2},{4,5},{7,6},{8,9},{11,10},{12,13},{15,14},{16,17},{19,... | collective-permute-start | bytes 860168 | tf_op jit(solution)/shard_map/ppermute | solution.py:522
  50.8 0.7 collective-permute-start.15
  51.6 0.1 pad_maximum_fusion
  51.7 2.3 %collective-permute-start.13 = (bf16[4,112,512]{2,1,0:T(8,128)(2,1)S(1)}, bf16[4,112,512]{2,1,0:T(8,128)(2,1)S(1)}, u32[]{:S(2)}, u32[]{:S(2)}) collective-permute-start(bf16[4,112,512]{2,1,0:T(8,128)(2,1)S(1)} %pad_maximum_fusion), channel_id=1, source_target_pairs={{0,4},{4,0},{8,12},{12,8},{16,20},{20,16},{24,28},{28,24},{1,5},{5... | collective-permute-start | bytes 1376264 | tf_op jit(solution)/shard_map/ppermute | solution.py:420
  54.1 2.1 %collective-permute-start.16 = (bf16[4,112,512]{2,1,0:T(8,128)(2,1)S(1)}, bf16[4,112,512]{2,1,0:T(8,128)(2,1)S(1)}, u32[]{:S(2)}, u32[]{:S(2)}) collective-permute-start(bf16[4,112,512]{2,1,0:T(8,128)(2,1)S(1)} %pad_maximum_fusion.1), channel_id=1, source_target_pairs={{4,8},{12,16},{20,24},{8,4},{16,12},{24,20},{5,9},{13,17},{21,25},... | collective-permute-start | bytes 1376264 | tf_op jit(solution)/shard_map/ppermute | solution.py:421
  56.2 0.3 collective-permute-done.14.refs_0_
  56.4 0.6 project_2.2
  57.1 6.6 %collective-permute-start.18 = (bf16[1120,128]{1,0:T(8,128)(2,1)S(1)}, bf16[1120,128]{1,0:T(8,128)(2,1)S(1)}, u32[]{:S(2)}, u32[]{:S(2)}) collective-permute-start(bf16[1120,128]{1,0:T(8,128)(2,1)S(1)} %project_2.2), channel_id=1, source_target_pairs={{0,2},{1,3},{2,0},{3,1},{4,6},{5,7},{6,4},{7,5},{8,10},{9,11},{10,... | collective-permute-start | bytes 860168 | tf_op jit(solution)/shard_map/ppermute | solution.py:530
  63.7 0.6 project_1.2
  64.3 3.1 %expand_own.3.refs_2_ = f32[2,192,1400]{2,1,0:T(8,128)S(1)} custom-call(bf16[2,112,512]{2,1,0:T(8,128)(2,1)S(1)} %get-tuple-element.48.refs_0_, bf16[2,112,512]{2,1,0:T(8,128)(2,1)S(1)} %collective-permute-done.5.refs_1_, bf16[2,112,512]{2,1,0:T(8,128)(2,1)S(1)} %collective-permute-done.6.refs_2_, bf16[2,112,512]{2,1,0:T(8,128)(2,1)S(1)} %collective-permute-done.7.refs_3_, ...), custom_call_target="tpu_custom_call" | custom-call | flops 1000 | bytes 1000 | tf_op jit(solution)/shard_map/expand_own/pallas_call | solution.py:473
  67.4 0.1 collective-permute-start.19
  67.5 5.2 %expand_conv.3.hidden_ref = bf16[192,1400]{1,0:T(8,128)(2,1)S(1)} custom-call(bf16[4,112,512]{2,1,0:T(8,128)(2,1)S(1)} %collective-permute-done.13.refs_0_, bf16[4,112,512]{2,1,0:T(8,128)(2,1)S(1)} %collective-permute-done.16.refs_1_, f32[2,192,1400]{2,1,0:T(8,128)S(1)} %expand_own.3.refs_2_, f32[4,96,128]{2,1,0:T(8,128)S(1)} %get-tuple-element.33.refs_4_.refs_3_.mask_ref, ...), custom_call_target="tpu_custom_call" | custom-call | flops 1000 | bytes 1000 | tf_op jit(solution)/shard_map/expand_conv/pallas_call | solution.py:489
  72.6 0.7 project_3.3
  73.3 3.9 %collective-permute-start.17 = (bf16[848,128]{1,0:T(8,128)(2,1)S(1)}, bf16[848,128]{1,0:T(8,128)(2,1)S(1)}, u32[]{:S(2)}, u32[]{:S(2)}) collective-permute-start(bf16[848,128]{1,0:T(8,128)(2,1)S(1)} %project_3.3), channel_id=1, source_target_pairs={{0,1},{3,2},{4,5},{7,6},{8,9},{11,10},{12,13},{15,14},{16,17},{19,... | collective-permute-start | bytes 651272 | tf_op jit(solution)/shard_map/ppermute | solution.py:522
  77.3 0.7 collective-permute-start.21
  78.0 0.7 project_0.2.share_ref
  78.6 3.6 %collective-permute-done.19.refs_1_ = bf16[1120,128]{1,0:T(8,128)(2,1)S(1)} collective-permute-done((bf16[1120,128]{1,0:T(8,128)(2,1)S(1)}, bf16[1120,128]{1,0:T(8,128)(2,1)S(1)}, u32[]{:S(2)}, u32[]{:S(2)}) %collective-permute-start.19) | collective-permute-done | bytes 286752 | tf_op jit(solution)/shard_map/ppermute | solution.py:532
  82.3 0.8 finish.2.refs_2_
  83.1 0.7 project_2.3
  83.8 0.1 collective-permute-start.20
  83.8 0.7 project_1.3
  84.5 1.7 %collective-permute-start.22 = (bf16[848,128]{1,0:T(8,128)(2,1)S(1)}, bf16[848,128]{1,0:T(8,128)(2,1)S(1)}, u32[]{:S(2)}, u32[]{:S(2)}) collective-permute-start(bf16[848,128]{1,0:T(8,128)(2,1)S(1)} %project_1.3), channel_id=1, source_target_pairs={{0,1},{1,0},{2,3},{3,2},{4,5},{5,4},{6,7},{7,6},{8,9},{9,8},{10,11... | collective-permute-start | bytes 651272 | tf_op jit(solution)/shard_map/ppermute | solution.py:532
  86.3 10.4 %collective-permute-done.20.unit_ref = bf16[848,128]{1,0:T(8,128)(2,1)S(1)} collective-permute-done((bf16[848,128]{1,0:T(8,128)(2,1)S(1)}, bf16[848,128]{1,0:T(8,128)(2,1)S(1)}, u32[]{:S(2)}, u32[]{:S(2)}) %collective-permute-start.20) | collective-permute-done | bytes 217120 | tf_op jit(solution)/shard_map/ppermute | solution.py:530
  96.6 0.6 project_0.3.share_ref
  97.3 1.7 %finish.3 = bf16[4,2,64,560]{3,2,1,0:T(8,128)(2,1)} custom-call(s32[4]{0:T(128)S(1)} %copy-done.5, f32[4,96,128]{2,1,0:T(8,128)S(1)} %get-tuple-element.33.refs_4_.refs_3_.mask_ref, f32[560,192]{1,0:T(8,128)S(1)} %project_0.3.share_ref, bf16[848,128]{1,0:T(8,128)(2,1)S(1)} %collective-permute-done.21.refs_0_, ...), custom_call_target="tpu_custom_call" | custom-call | flops 99999997952 | bytes 1000000000 | tf_op jit(solution)/shard_map/finish/pallas_call | solution.py:543
  (45 shorter events, 0.4 us)
Async XLA Ops:
  0.0 1.1 %copy-start = (bf16[4,2,64,560]{3,2,1,0:T(8,128)(2,1)S(1)}, bf16[4,2,64,560]{3,2,1,0:T(8,128)(2,1)}, u32[]{:S(2)}) copy-start(bf16[4,2,64,560]{3,2,1,0:T(8,128)(2,1)} %x_ref.1) | copy-start | bytes 1720324
  1.1 0.7 copy-start.4
  2.4 16.1 %collective-permute-start = (bf16[2,144,512]{2,1,0:T(8,128)(2,1)S(1)}, bf16[2,144,512]{2,1,0:T(8,128)(2,1)S(1)}, u32[]{:S(2)}, u32[]{:S(2)}) collective-permute-start(bf16[2,144,512]{2,1,0:T(8,128)(2,1)S(1)} %get-tuple-element.35.refs_0_), channel_id=1, source_target_pairs={{0,2},{1,3},{2,0},{3,1},{4,6},{5,7},{6,4},{7,5},{8,10},{9,11},{10,... | collective-permute-start | bytes 884744 | tf_op jit(solution)/shard_map/ppermute | solution.py:425
  5.1 9.8 %collective-permute-start.1 = (bf16[1,144,512]{2,1,0:T(8,128)(2,1)S(1)}, bf16[1,144,512]{2,1,0:T(8,128)(2,1)S(1)}, u32[]{:S(2)}, u32[]{:S(2)}) collective-permute-start(bf16[1,144,512]{2,1,0:T(8,128)(2,1)S(1)} %get-tuple-element.60), channel_id=1, source_target_pairs={{0,4},{4,0},{8,12},{12,8},{16,20},{20,16},{24,28},{28,24},{1,5},{5... | collective-permute-start | bytes 442376 | tf_op jit(solution)/shard_map/ppermute | solution.py:420
  5.2 21.6 %copy-start.1 = (f32[3,3,2,1400]{3,2,1,0:T(2,128)S(1)}, f32[3,3,2,1400]{3,2,1,0:T(2,128)}, u32[]{:S(2)}) copy-start(f32[3,3,2,1400]{3,2,1,0:T(2,128)} %dw_ref) | copy-start | bytes 302404
  5.2 21.6 %copy-start.2 = (f32[2,1400]{1,0:T(2,128)S(1)}, f32[2,1400]{1,0:T(2,128)}, u32[]{:S(2)}) copy-start(f32[2,1400]{1,0:T(2,128)} %eb_ref.1) | copy-start | bytes 33604
  5.2 21.6 %copy-start.3 = (f32[2,1400]{1,0:T(2,128)S(1)}, f32[2,1400]{1,0:T(2,128)}, u32[]{:S(2)}) copy-start(f32[2,1400]{1,0:T(2,128)} %db_ref.1) | copy-start | bytes 33604
  5.2 21.6 %copy-start.6 = (s32[4]{0:T(128)S(1)}, s32[4]{0:T(128)}, u32[]{:S(2)}) copy-start(s32[4]{0:T(128)} %height_ref.1) | copy-start | bytes 52
  5.2 9.6 %collective-permute-start.2 = (bf16[1,144,512]{2,1,0:T(8,128)(2,1)S(1)}, bf16[1,144,512]{2,1,0:T(8,128)(2,1)S(1)}, u32[]{:S(2)}, u32[]{:S(2)}) collective-permute-start(bf16[1,144,512]{2,1,0:T(8,128)(2,1)S(1)} %get-tuple-element.59), channel_id=1, source_target_pairs={{4,8},{12,16},{20,24},{8,4},{16,12},{24,20},{5,9},{13,17},{21,25},... | collective-permute-start | bytes 442376 | tf_op jit(solution)/shard_map/ppermute | solution.py:421
  7.9 15.1 %collective-permute-start.8 = (bf16[2,144,512]{2,1,0:T(8,128)(2,1)S(1)}, bf16[2,144,512]{2,1,0:T(8,128)(2,1)S(1)}, u32[]{:S(2)}, u32[]{:S(2)}) collective-permute-start(bf16[2,144,512]{2,1,0:T(8,128)(2,1)S(1)} %get-tuple-element.35.refs_0_), channel_id=1, source_target_pairs={{0,1},{1,0},{2,3},{3,2},{4,5},{5,4},{6,7},{7,6},{8,9},{9,8},{10,11... | collective-permute-start | bytes 884744 | tf_op jit(solution)/shard_map/ppermute | solution.py:426
  18.5 8.8 %collective-permute-start.3 = (bf16[2,144,512]{2,1,0:T(8,128)(2,1)S(1)}, bf16[2,144,512]{2,1,0:T(8,128)(2,1)S(1)}, u32[]{:S(2)}, u32[]{:S(2)}) collective-permute-start(bf16[2,144,512]{2,1,0:T(8,128)(2,1)S(1)} %get-tuple-element.35.refs_0_), channel_id=1, source_target_pairs={{1,2},{2,1},{5,6},{6,5},{9,10},{10,9},{13,14},{14,13},{17,18},{18,... | collective-permute-start | bytes 884744 | tf_op jit(solution)/shard_map/ppermute | solution.py:427
  19.2 10.3 %collective-permute-start.4 = (bf16[2,144,512]{2,1,0:T(8,128)(2,1)S(1)}, bf16[2,144,512]{2,1,0:T(8,128)(2,1)S(1)}, u32[]{:S(2)}, u32[]{:S(2)}) collective-permute-start(bf16[2,144,512]{2,1,0:T(8,128)(2,1)S(1)} %collective-permute-done.refs_2_), channel_id=1, source_target_pairs={{2,3},{1,0},{6,7},{5,4},{10,11},{9,8},{14,15},{13,12},{18,19},{17,... | collective-permute-start | bytes 884744 | tf_op jit(solution)/shard_map/ppermute | solution.py:428
  23.0 11.2 %collective-permute-start.11 = (bf16[2,144,512]{2,1,0:T(8,128)(2,1)S(1)}, bf16[2,144,512]{2,1,0:T(8,128)(2,1)S(1)}, u32[]{:S(2)}, u32[]{:S(2)}) collective-permute-start(bf16[2,144,512]{2,1,0:T(8,128)(2,1)S(1)} %pad_maximum_fusion.3), channel_id=1, source_target_pairs={{4,8},{12,16},{20,24},{8,4},{16,12},{24,20},{5,9},{13,17},{21,25},... | collective-permute-start | bytes 884744 | tf_op jit(solution)/shard_map/ppermute | solution.py:421
  25.0 9.2 %collective-permute-start.9 = (bf16[2,144,512]{2,1,0:T(8,128)(2,1)S(1)}, bf16[2,144,512]{2,1,0:T(8,128)(2,1)S(1)}, u32[]{:S(2)}, u32[]{:S(2)}) collective-permute-start(bf16[2,144,512]{2,1,0:T(8,128)(2,1)S(1)} %pad_maximum_fusion.2), channel_id=1, source_target_pairs={{0,4},{4,0},{8,12},{12,8},{16,20},{20,16},{24,28},{28,24},{1,5},{5... | collective-permute-start | bytes 884744 | tf_op jit(solution)/shard_map/ppermute | solution.py:420
  29.6 21.9 %collective-permute-start.5 = (bf16[2,112,512]{2,1,0:T(8,128)(2,1)S(1)}, bf16[2,112,512]{2,1,0:T(8,128)(2,1)S(1)}, u32[]{:S(2)}, u32[]{:S(2)}) collective-permute-start(bf16[2,112,512]{2,1,0:T(8,128)(2,1)S(1)} %get-tuple-element.48.refs_0_), channel_id=1, source_target_pairs={{0,1},{1,0},{2,3},{3,2},{4,5},{5,4},{6,7},{7,6},{8,9},{9,8},{10,11... | collective-permute-start | bytes 688136 | tf_op jit(solution)/shard_map/ppermute | solution.py:433
  30.1 21.4 %collective-permute-start.6 = (bf16[2,112,512]{2,1,0:T(8,128)(2,1)S(1)}, bf16[2,112,512]{2,1,0:T(8,128)(2,1)S(1)}, u32[]{:S(2)}, u32[]{:S(2)}) collective-permute-start(bf16[2,112,512]{2,1,0:T(8,128)(2,1)S(1)} %get-tuple-element.48.refs_0_), channel_id=1, source_target_pairs={{0,2},{1,3},{2,0},{3,1},{4,6},{5,7},{6,4},{7,5},{8,10},{9,11},{10,... | collective-permute-start | bytes 688136 | tf_op jit(solution)/shard_map/ppermute | solution.py:433
  34.2 17.3 %collective-permute-start.7 = (bf16[2,112,512]{2,1,0:T(8,128)(2,1)S(1)}, bf16[2,112,512]{2,1,0:T(8,128)(2,1)S(1)}, u32[]{:S(2)}, u32[]{:S(2)}) collective-permute-start(bf16[2,112,512]{2,1,0:T(8,128)(2,1)S(1)} %get-tuple-element.48.refs_0_), channel_id=1, source_target_pairs={{0,3},{1,2},{2,1},{3,0},{4,7},{5,6},{6,5},{7,4},{8,11},{9,10},{10,... | collective-permute-start | bytes 688136 | tf_op jit(solution)/shard_map/ppermute | solution.py:433
  34.2 6.6 %collective-permute-start.10 = (bf16[1,144,512]{2,1,0:T(8,128)(2,1)S(1)}, bf16[1,144,512]{2,1,0:T(8,128)(2,1)S(1)}, u32[]{:S(2)}, u32[]{:S(2)}) collective-permute-start(bf16[1,144,512]{2,1,0:T(8,128)(2,1)S(1)} %get-tuple-element.58), channel_id=1, source_target_pairs={{0,4},{4,0},{8,12},{12,8},{16,20},{20,16},{24,28},{28,24},{1,5},{5... | collective-permute-start | bytes 442376 | tf_op jit(solution)/shard_map/ppermute | solution.py:420
  34.2 6.6 %collective-permute-start.12 = (bf16[1,144,512]{2,1,0:T(8,128)(2,1)S(1)}, bf16[1,144,512]{2,1,0:T(8,128)(2,1)S(1)}, u32[]{:S(2)}, u32[]{:S(2)}) collective-permute-start(bf16[1,144,512]{2,1,0:T(8,128)(2,1)S(1)} %get-tuple-element.57), channel_id=1, source_target_pairs={{4,8},{12,16},{20,24},{8,4},{16,12},{24,20},{5,9},{13,17},{21,25},... | collective-permute-start | bytes 442376 | tf_op jit(solution)/shard_map/ppermute | solution.py:421
  36.8 10.9 %slice-start = ((s8[6307840]{0:T(1024)(128)(4,1)}), s8[4194304]{0:T(1024)(128)(4,1)S(1)}, s32[]{:S(2)}) async-start(s8[6307840]{0:T(1024)(128)(4,1)} %bitcast.1), calls=%async_computation | async-start | bytes 8388608
  40.8 6.9 %slice-start.1 = ((s8[6307840]{0:T(1024)(128)(4,1)}), s8[2113536]{0:T(1024)(128)(4,1)S(1)}, s32[]{:S(2)}) async-start(s8[6307840]{0:T(1024)(128)(4,1)} %bitcast.1), calls=%async_computation.1 | async-start | bytes 4227072
  48.3 8.1 %collective-permute-start.14 = (bf16[1120,128]{1,0:T(8,128)(2,1)S(1)}, bf16[1120,128]{1,0:T(8,128)(2,1)S(1)}, u32[]{:S(2)}, u32[]{:S(2)}) collective-permute-start(bf16[1120,128]{1,0:T(8,128)(2,1)S(1)} %project_3.2), channel_id=1, source_target_pairs={{0,1},{3,2},{4,5},{7,6},{8,9},{11,10},{12,13},{15,14},{16,17},{19,... | collective-permute-start | bytes 860168 | tf_op jit(solution)/shard_map/ppermute | solution.py:522
  50.8 5.6 %collective-permute-start.15 = (bf16[1120,128]{1,0:T(8,128)(2,1)S(1)}, bf16[1120,128]{1,0:T(8,128)(2,1)S(1)}, u32[]{:S(2)}, u32[]{:S(2)}) collective-permute-start(bf16[1120,128]{1,0:T(8,128)(2,1)S(1)} %project_3.2), channel_id=1, source_target_pairs={{1,2},{2,1},{5,6},{6,5},{9,10},{10,9},{13,14},{14,13},{17,18},{18,... | collective-permute-start | bytes 860168 | tf_op jit(solution)/shard_map/ppermute | solution.py:523
  51.7 15.8 %collective-permute-start.13 = (bf16[4,112,512]{2,1,0:T(8,128)(2,1)S(1)}, bf16[4,112,512]{2,1,0:T(8,128)(2,1)S(1)}, u32[]{:S(2)}, u32[]{:S(2)}) collective-permute-start(bf16[4,112,512]{2,1,0:T(8,128)(2,1)S(1)} %pad_maximum_fusion), channel_id=1, source_target_pairs={{0,4},{4,0},{8,12},{12,8},{16,20},{20,16},{24,28},{28,24},{1,5},{5... | collective-permute-start | bytes 1376264 | tf_op jit(solution)/shard_map/ppermute | solution.py:420
  54.1 13.4 %collective-permute-start.16 = (bf16[4,112,512]{2,1,0:T(8,128)(2,1)S(1)}, bf16[4,112,512]{2,1,0:T(8,128)(2,1)S(1)}, u32[]{:S(2)}, u32[]{:S(2)}) collective-permute-start(bf16[4,112,512]{2,1,0:T(8,128)(2,1)S(1)} %pad_maximum_fusion.1), channel_id=1, source_target_pairs={{4,8},{12,16},{20,24},{8,4},{16,12},{24,20},{5,9},{13,17},{21,25},... | collective-permute-start | bytes 1376264 | tf_op jit(solution)/shard_map/ppermute | solution.py:421
  57.1 20.9 %collective-permute-start.18 = (bf16[1120,128]{1,0:T(8,128)(2,1)S(1)}, bf16[1120,128]{1,0:T(8,128)(2,1)S(1)}, u32[]{:S(2)}, u32[]{:S(2)}) collective-permute-start(bf16[1120,128]{1,0:T(8,128)(2,1)S(1)} %project_2.2), channel_id=1, source_target_pairs={{0,2},{1,3},{2,0},{3,1},{4,6},{5,7},{6,4},{7,5},{8,10},{9,11},{10,... | collective-permute-start | bytes 860168 | tf_op jit(solution)/shard_map/ppermute | solution.py:530
  67.4 14.9 %collective-permute-start.19 = (bf16[1120,128]{1,0:T(8,128)(2,1)S(1)}, bf16[1120,128]{1,0:T(8,128)(2,1)S(1)}, u32[]{:S(2)}, u32[]{:S(2)}) collective-permute-start(bf16[1120,128]{1,0:T(8,128)(2,1)S(1)} %project_1.2), channel_id=1, source_target_pairs={{0,1},{1,0},{2,3},{3,2},{4,5},{5,4},{6,7},{7,6},{8,9},{9,8},{10,11... | collective-permute-start | bytes 860168 | tf_op jit(solution)/shard_map/ppermute | solution.py:532
  73.3 8.9 %copy-start.5 = (s32[4]{0:T(128)S(1)}, s32[4]{0:T(128)}, u32[]{:S(2)}) copy-start(s32[4]{0:T(128)} %width_ref.7) | copy-start | bytes 52
  73.3 9.7 %collective-permute-start.17 = (bf16[848,128]{1,0:T(8,128)(2,1)S(1)}, bf16[848,128]{1,0:T(8,128)(2,1)S(1)}, u32[]{:S(2)}, u32[]{:S(2)}) collective-permute-start(bf16[848,128]{1,0:T(8,128)(2,1)S(1)} %project_3.3), channel_id=1, source_target_pairs={{0,1},{3,2},{4,5},{7,6},{8,9},{11,10},{12,13},{15,14},{16,17},{19,... | collective-permute-start | bytes 651272 | tf_op jit(solution)/shard_map/ppermute | solution.py:522
  77.3 7.3 %collective-permute-start.21 = (bf16[848,128]{1,0:T(8,128)(2,1)S(1)}, bf16[848,128]{1,0:T(8,128)(2,1)S(1)}, u32[]{:S(2)}, u32[]{:S(2)}) collective-permute-start(bf16[848,128]{1,0:T(8,128)(2,1)S(1)} %project_3.3), channel_id=1, source_target_pairs={{1,2},{2,1},{5,6},{6,5},{9,10},{10,9},{13,14},{14,13},{17,18},{18,... | collective-permute-start | bytes 651272 | tf_op jit(solution)/shard_map/ppermute | solution.py:523
  83.8 12.9 %collective-permute-start.20 = (bf16[848,128]{1,0:T(8,128)(2,1)S(1)}, bf16[848,128]{1,0:T(8,128)(2,1)S(1)}, u32[]{:S(2)}, u32[]{:S(2)}) collective-permute-start(bf16[848,128]{1,0:T(8,128)(2,1)S(1)} %project_2.3), channel_id=1, source_target_pairs={{0,2},{1,3},{2,0},{3,1},{4,6},{5,7},{6,4},{7,5},{8,10},{9,11},{10,... | collective-permute-start | bytes 651272 | tf_op jit(solution)/shard_map/ppermute | solution.py:530
  84.5 12.7 %collective-permute-start.22 = (bf16[848,128]{1,0:T(8,128)(2,1)S(1)}, bf16[848,128]{1,0:T(8,128)(2,1)S(1)}, u32[]{:S(2)}, u32[]{:S(2)}) collective-permute-start(bf16[848,128]{1,0:T(8,128)(2,1)S(1)} %project_1.3), channel_id=1, source_target_pairs={{0,1},{1,0},{2,3},{3,2},{4,5},{5,4},{6,7},{7,6},{8,9},{9,8},{10,11... | collective-permute-start | bytes 651272 | tf_op jit(solution)/shard_map/ppermute | solution.py:532

commit v2 on v1

--- a/solution.py
+++ b/solution.py
@@ -460,15 +460,17 @@
     )(clip_height, clip_width, taps, expand_bias, depth_bias)
     groups = ((0,), (1, 2), (3,))
     inner, outer = send_rows(*edge_rows(own[:1], groups[:1]))
-    packets = relay(own[0], parameters, token, *inner, *outer)
+    early = send_rows(*edge_rows(own[1:], groups[:1]))
+    packets = relay(own[0], parameters, token, *inner, *outer, *early[0], *early[1])
     edges = edge_rows(packets, groups[1:])
     later = send_rows(*edges)
     inner, outer = inner + later[0], outer + later[1]
     upcoming = direct(after(own[1], edges[0][-1], edges[1][-1]))
     for number, chunk in enumerate(chunks):
         if number:
-            packets, groups = list(lax.optimization_barrier((*upcoming, hidden))[:shards]), ((0, 1, 2, 3),)
-            inner, outer = send_rows(*edge_rows(packets, groups))
+            packets, groups = list(lax.optimization_barrier((*upcoming, hidden))[:shards]), ((0,), (1, 2, 3))
+            later = send_rows(*edge_rows(packets, groups[1:]))
+            inner, outer = early[0] + later[0], early[1] + later[1]
             packets[0] = after(packets[0], far)
         rows = pl.pallas_call(
             functools.partial(own_kernel, chunk=chunk, shards=shards),

time: 99.4 us -> 98.7 us (level)
  waiting for transfers between devices: 22.6 us -> 17.6 us
  starting transfers between devices: 40.3 us -> 43.7 us
    ppermute x1, waiting for transfers between devices: 3.69 us -> 0.03 us  [relay(): second = lax.ppermute(mine, 'tensor', two_off)]
    ppermute x4 -> x5, starting transfers between devices: 4.1 us -> 6.6 us  [send_rows(): lax.ppermute(x, 'row', sibling)]
    ppermute x4 -> x5, starting transfers between devices: 9.19 us -> 11.7 us  [send_rows(): lax.ppermute(x, 'row', beyond)]
    ppermute x2, waiting for transfers between devices: 3.64 us -> 1.29 us  [on_device_packed(): arrived = [across, lax.ppermute(close, 'tensor', near)]]
    ppermute x1, waiting for transfers between devices: 2.42 us -> 4.2 us  [relay(): first = lax.ppermute(mine, 'tensor', near)]
    ppermute x2, waiting for transfers between devices: 10.4 us -> 8.62 us  [on_device_packed(): distant = lax.ppermute(last_unit, 'tensor', two_off)]
    ppermute x2, starting transfers between devices: 1.8 us -> 0.14 us  [on_device_packed(): arrived = [across, lax.ppermute(close, 'tensor', near)]]
    ppermute x2, waiting for transfers between devices: 0.26 us -> 1.55 us  [on_device_packed(): relayed = lax.ppermute(far, 'tensor', from_end)]
  transfers between devices with their start and end apart: 23 -> 25, of which waited for: 6 -> 5; matrix products, arithmetic and copies ran while one was open for 0% -> 0% of each run, Pallas kernels for 31% -> 32%
where the time goes in v2:
time: 98.7 us; the launch traced here: 97.3 us
  starting transfers between devices  43.7 us (44%)
  Pallas kernels  33.4 us (34%)
  waiting for transfers between devices  17.6 us (18%)
  local copies, waits for them, and re-layouts  1.93 us (2%)
    pallas_call x2, Pallas kernels, on_device_packed(): pl.pallas_call(functools.partial(hidden_kernel, chunk=chunk, shards=shard...  12 us
    ppermute x5, starting transfers between devices, send_rows(): lax.ppermute(x, 'row', beyond)  11.7 us
    ppermute x2, waiting for transfers between devices, on_device_packed(): distant = lax.ppermute(last_unit, 'tensor', two_off)  8.62 us
    ppermute x2, starting transfers between devices, on_device_packed(): distant = lax.ppermute(last_unit, 'tensor', two_off)  7.69 us
    pallas_call x2, Pallas kernels, on_device_packed(): pl.pallas_call(functools.partial(own_kernel, chunk=chunk, shards=shards),...  7.05 us
    ppermute x5, starting transfers between devices, send_rows(): lax.ppermute(x, 'row', sibling)  6.6 us
    ppermute x2, starting transfers between devices, on_device_packed(): relayed = lax.ppermute(far, 'tensor', from_end)  5.54 us
    pallas_call x1, Pallas kernels, on_device_packed(): pl.pallas_call(functools.partial(load_kernel, shards=shards, depth=depth)...  5.33 us
  transfers between devices with their start and end apart: 25, of which 5 were waited for; matrix products, arithmetic and copies ran while one was open for 0% of the time, Pallas kernels for 32%

profile of v2, /device:TPU:2, one launch (start us, length us, event | category | flops | bytes accessed | tf_op | source)
XLA Modules:
  0.0 97.3 jit_solution(3923603616538096498)
XLA Ops:
  0.0 1.1 %copy-done = bf16[4,2,64,560]{3,2,1,0:T(8,128)(2,1)S(1)} copy-done((bf16[4,2,64,560]{3,2,1,0:T(8,128)(2,1)S(1)}, bf16[4,2,64,560]{3,2,1,0:T(8,128)(2,1)}, u32[]{:S(2)}) %copy-start) | copy-done | bytes 573464
  1.1 0.7 copy-done.4
  1.7 0.7 pack.1
  2.4 2.7 %collective-permute-start.3 = (bf16[2,144,512]{2,1,0:T(8,128)(2,1)S(1)}, bf16[2,144,512]{2,1,0:T(8,128)(2,1)S(1)}, u32[]{:S(2)}, u32[]{:S(2)}) collective-permute-start(bf16[2,144,512]{2,1,0:T(8,128)(2,1)S(1)} %get-tuple-element.35.refs_0_), channel_id=1, source_target_pairs={{0,2},{1,3},{2,0},{3,1},{4,6},{5,7},{6,4},{7,5},{8,10},{9,11},{10,... | collective-permute-start | bytes 884744 | tf_op jit(solution)/shard_map/ppermute | solution.py:425
  5.1 0.1 collective-permute-start
  5.2 0.6 collective-permute-start.1
  5.7 2.1 %collective-permute-start.5 = (bf16[1,144,512]{2,1,0:T(8,128)(2,1)S(1)}, bf16[1,144,512]{2,1,0:T(8,128)(2,1)S(1)}, u32[]{:S(2)}, u32[]{:S(2)}) collective-permute-start(bf16[1,144,512]{2,1,0:T(8,128)(2,1)S(1)} %get-tuple-element.59), channel_id=1, source_target_pairs={{4,8},{12,16},{20,24},{8,4},{16,12},{24,20},{5,9},{13,17},{21,25},... | collective-permute-start | bytes 442376 | tf_op jit(solution)/shard_map/ppermute | solution.py:421
  7.9 3.6 %collective-permute-start.6 = (bf16[1,112,512]{2,1,0:T(8,128)(2,1)S(1)}, bf16[1,112,512]{2,1,0:T(8,128)(2,1)S(1)}, u32[]{:S(2)}, u32[]{:S(2)}) collective-permute-start(bf16[1,112,512]{2,1,0:T(8,128)(2,1)S(1)} %get-tuple-element.67), channel_id=1, source_target_pairs={{4,8},{12,16},{20,24},{8,4},{16,12},{24,20},{5,9},{13,17},{21,25},... | collective-permute-start | bytes 344072 | tf_op jit(solution)/shard_map/ppermute | solution.py:421
  11.5 1.6 %collective-permute-start.2 = (bf16[2,144,512]{2,1,0:T(8,128)(2,1)S(1)}, bf16[2,144,512]{2,1,0:T(8,128)(2,1)S(1)}, u32[]{:S(2)}, u32[]{:S(2)}) collective-permute-start(bf16[2,144,512]{2,1,0:T(8,128)(2,1)S(1)} %get-tuple-element.35.refs_0_), channel_id=1, source_target_pairs={{0,1},{1,0},{2,3},{3,2},{4,5},{5,4},{6,7},{7,6},{8,9},{9,8},{10,11... | collective-permute-start | bytes 884744 | tf_op jit(solution)/shard_map/ppermute | solution.py:426
  13.1 5.3 %load_weights.1 = (bf16[2,2240,1400]{2,1,0:T(8,128)(2,1)S(1)}, f32[8,128]{1,0:T(8,128)}) custom-call(bf16[2,2240,1400]{2,1,0:T(8,128)(2,1)} %w_ref), custom_call_target="tpu_custom_call" | custom-call | tf_op jit(solution)/shard_map/load_weights/pallas_call | solution.py:438
  18.5 0.7 collective-permute-start.7
  19.2 1.3 %collective-permute-start.8 = (bf16[2,144,512]{2,1,0:T(8,128)(2,1)S(1)}, bf16[2,144,512]{2,1,0:T(8,128)(2,1)S(1)}, u32[]{:S(2)}, u32[]{:S(2)}) collective-permute-start(bf16[2,144,512]{2,1,0:T(8,128)(2,1)S(1)} %collective-permute-done.3.refs_2_), channel_id=1, source_target_pairs={{2,3},{1,0},{6,7},{5,4},{10,11},{9,8},{14,15},{13,12},{18,19},{17,... | collective-permute-start | bytes 884744 | tf_op jit(solution)/shard_map/ppermute | solution.py:428
  20.5 4.2 %collective-permute-done.2.refs_1_ = bf16[2,144,512]{2,1,0:T(8,128)(2,1)S(1)} collective-permute-done((bf16[2,144,512]{2,1,0:T(8,128)(2,1)S(1)}, bf16[2,144,512]{2,1,0:T(8,128)(2,1)S(1)}, u32[]{:S(2)}, u32[]{:S(2)}) %collective-permute-start.2) | collective-permute-done | bytes 294944 | tf_op jit(solution)/shard_map/ppermute | solution.py:426
  24.8 1.9 %collective-permute-start.10 = (bf16[2,144,512]{2,1,0:T(8,128)(2,1)S(1)}, bf16[2,144,512]{2,1,0:T(8,128)(2,1)S(1)}, u32[]{:S(2)}, u32[]{:S(2)}) collective-permute-start(bf16[2,144,512]{2,1,0:T(8,128)(2,1)S(1)} %pad_maximum_fusion.3), channel_id=1, source_target_pairs={{4,8},{12,16},{20,24},{8,4},{16,12},{24,20},{5,9},{13,17},{21,25},... | collective-permute-start | bytes 884744 | tf_op jit(solution)/shard_map/ppermute | solution.py:421
  26.8 1.8 %collective-permute-start.4 = (bf16[2,144,512]{2,1,0:T(8,128)(2,1)S(1)}, bf16[2,144,512]{2,1,0:T(8,128)(2,1)S(1)}, u32[]{:S(2)}, u32[]{:S(2)}) collective-permute-start(bf16[2,144,512]{2,1,0:T(8,128)(2,1)S(1)} %pad_maximum_fusion.2), channel_id=1, source_target_pairs={{0,4},{4,0},{8,12},{12,8},{16,20},{20,16},{24,28},{28,24},{1,5},{5... | collective-permute-start | bytes 884744 | tf_op jit(solution)/shard_map/ppermute | solution.py:420
  28.5 0.6 tables.1
  29.2 1.9 %collective-permute-done.8 = bf16[2,144,512]{2,1,0:T(8,128)(2,1)S(1)} collective-permute-done((bf16[2,144,512]{2,1,0:T(8,128)(2,1)S(1)}, bf16[2,144,512]{2,1,0:T(8,128)(2,1)S(1)}, u32[]{:S(2)}, u32[]{:S(2)}) %collective-permute-start.8) | collective-permute-done | bytes 294944 | tf_op jit(solution)/shard_map/ppermute | solution.py:428
  31.1 0.1 add.3.refs_3_
  31.2 0.1 collective-permute-start.14
  31.3 4.0 %collective-permute-start.15 = (bf16[2,112,512]{2,1,0:T(8,128)(2,1)S(1)}, bf16[2,112,512]{2,1,0:T(8,128)(2,1)S(1)}, u32[]{:S(2)}, u32[]{:S(2)}) collective-permute-start(bf16[2,112,512]{2,1,0:T(8,128)(2,1)S(1)} %get-tuple-element.48.refs_0_), channel_id=1, source_target_pairs={{0,2},{1,3},{2,0},{3,1},{4,6},{5,7},{6,4},{7,5},{8,10},{9,11},{10,... | collective-permute-start | bytes 688136 | tf_op jit(solution)/shard_map/ppermute | solution.py:433
  35.3 0.3 collective-permute-start.16
  35.6 1.9 %collective-permute-start.11 = (bf16[1,144,512]{2,1,0:T(8,128)(2,1)S(1)}, bf16[1,144,512]{2,1,0:T(8,128)(2,1)S(1)}, u32[]{:S(2)}, u32[]{:S(2)}) collective-permute-start(bf16[1,144,512]{2,1,0:T(8,128)(2,1)S(1)} %get-tuple-element.53), channel_id=1, source_target_pairs={{4,8},{12,16},{20,24},{8,4},{16,12},{24,20},{5,9},{13,17},{21,25},... | collective-permute-start | bytes 442376 | tf_op jit(solution)/shard_map/ppermute | solution.py:421
  37.6 2.0 %collective-permute-start.9 = (bf16[1,144,512]{2,1,0:T(8,128)(2,1)S(1)}, bf16[1,144,512]{2,1,0:T(8,128)(2,1)S(1)}, u32[]{:S(2)}, u32[]{:S(2)}) collective-permute-start(bf16[1,144,512]{2,1,0:T(8,128)(2,1)S(1)} %get-tuple-element.54), channel_id=1, source_target_pairs={{0,4},{4,0},{8,12},{12,8},{16,20},{20,16},{24,28},{28,24},{1,5},{5... | collective-permute-start | bytes 442376 | tf_op jit(solution)/shard_map/ppermute | solution.py:420
  39.6 4.0 %expand_own.2.refs_6_ = f32[2,256,1400]{2,1,0:T(8,128)S(1)} custom-call(bf16[2,144,512]{2,1,0:T(8,128)(2,1)S(1)} %get-tuple-element.35.refs_0_, bf16[2,144,512]{2,1,0:T(8,128)(2,1)S(1)} %collective-permute-done.2.refs_1_, bf16[2,144,512]{2,1,0:T(8,128)(2,1)S(1)} %collective-permute-done.3.refs_2_, bf16[2,144,512]{2,1,0:T(8,128)(2,1)S(1)} %add.3.refs_3_, ...), custom_call_target="tpu_custom_call" | custom-call | flops 1000 | bytes 1000 | tf_op jit(solution)/shard_map/expand_own/pallas_call | solution.py:475
  43.6 6.8 %expand_conv.2.hidden_ref = bf16[256,1400]{1,0:T(8,128)(2,1)S(1)} custom-call(bf16[1,144,512]{2,1,0:T(8,128)(2,1)S(1)} %collective-permute-done.1.refs_0_, bf16[2,144,512]{2,1,0:T(8,128)(2,1)S(1)} %collective-permute-done.4.refs_1_, bf16[1,144,512]{2,1,0:T(8,128)(2,1)S(1)} %collective-permute-done.9.refs_2_, ...), custom_call_target="tpu_custom_call" | custom-call | flops 1000 | bytes 1000 | tf_op jit(solution)/shard_map/expand_conv/pallas_call | solution.py:491
  50.5 0.6 project_3.2
  51.1 1.6 %collective-permute-start.12 = (bf16[1120,128]{1,0:T(8,128)(2,1)S(1)}, bf16[1120,128]{1,0:T(8,128)(2,1)S(1)}, u32[]{:S(2)}, u32[]{:S(2)}) collective-permute-start(bf16[1120,128]{1,0:T(8,128)(2,1)S(1)} %project_3.2), channel_id=1, source_target_pairs={{0,1},{3,2},{4,5},{7,6},{8,9},{11,10},{12,13},{15,14},{16,17},{19,... | collective-permute-start | bytes 860168 | tf_op jit(solution)/shard_map/ppermute | solution.py:524
  52.8 0.7 collective-permute-start.13
  53.6 2.1 %collective-permute-start.18 = (bf16[3,112,512]{2,1,0:T(8,128)(2,1)S(1)}, bf16[3,112,512]{2,1,0:T(8,128)(2,1)S(1)}, u32[]{:S(2)}, u32[]{:S(2)}) collective-permute-start(bf16[3,112,512]{2,1,0:T(8,128)(2,1)S(1)} %pad_maximum_fusion.1), channel_id=1, source_target_pairs={{4,8},{12,16},{20,24},{8,4},{16,12},{24,20},{5,9},{13,17},{21,25},... | collective-permute-start | bytes 1032200 | tf_op jit(solution)/shard_map/ppermute | solution.py:421
  55.8 2.2 %collective-permute-start.17 = (bf16[3,112,512]{2,1,0:T(8,128)(2,1)S(1)}, bf16[3,112,512]{2,1,0:T(8,128)(2,1)S(1)}, u32[]{:S(2)}, u32[]{:S(2)}) collective-permute-start(bf16[3,112,512]{2,1,0:T(8,128)(2,1)S(1)} %pad_maximum_fusion), channel_id=1, source_target_pairs={{0,4},{4,0},{8,12},{12,8},{16,20},{20,16},{24,28},{28,24},{1,5},{5... | collective-permute-start | bytes 1032200 | tf_op jit(solution)/shard_map/ppermute | solution.py:420
  58.0 1.5 %collective-permute-done.12.refs_0_ = bf16[1120,128]{1,0:T(8,128)(2,1)S(1)} collective-permute-done((bf16[1120,128]{1,0:T(8,128)(2,1)S(1)}, bf16[1120,128]{1,0:T(8,128)(2,1)S(1)}, u32[]{:S(2)}, u32[]{:S(2)}) %collective-permute-start.12) | collective-permute-done | bytes 286752 | tf_op jit(solution)/shard_map/ppermute | solution.py:524
  59.5 0.6 project_2.2
  60.2 5.2 %collective-permute-start.20 = (bf16[1120,128]{1,0:T(8,128)(2,1)S(1)}, bf16[1120,128]{1,0:T(8,128)(2,1)S(1)}, u32[]{:S(2)}, u32[]{:S(2)}) collective-permute-start(bf16[1120,128]{1,0:T(8,128)(2,1)S(1)} %project_2.2), channel_id=1, source_target_pairs={{0,2},{1,3},{2,0},{3,1},{4,6},{5,7},{6,4},{7,5},{8,10},{9,11},{10,... | collective-permute-start | bytes 860168 | tf_op jit(solution)/shard_map/ppermute | solution.py:532
  65.4 0.6 project_1.2
  66.0 3.1 %expand_own.3.refs_4_ = f32[2,192,1400]{2,1,0:T(8,128)S(1)} custom-call(bf16[2,112,512]{2,1,0:T(8,128)(2,1)S(1)} %get-tuple-element.48.refs_0_, bf16[2,112,512]{2,1,0:T(8,128)(2,1)S(1)} %collective-permute-done.14.refs_1_, bf16[2,112,512]{2,1,0:T(8,128)(2,1)S(1)} %collective-permute-done.15.refs_2_, ...), custom_call_target="tpu_custom_call" | custom-call | flops 1000 | bytes 1000 | tf_op jit(solution)/shard_map/expand_own/pallas_call | solution.py:475
  69.2 5.1 %expand_conv.3.hidden_ref = bf16[192,1400]{1,0:T(8,128)(2,1)S(1)} custom-call(bf16[1,112,512]{2,1,0:T(8,128)(2,1)S(1)} %collective-permute-done.refs_0_, bf16[3,112,512]{2,1,0:T(8,128)(2,1)S(1)} %collective-permute-done.17.refs_1_, bf16[1,112,512]{2,1,0:T(8,128)(2,1)S(1)} %collective-permute-done.6.refs_2_, ...), custom_call_target="tpu_custom_call" | custom-call | flops 1000 | bytes 1000 | tf_op jit(solution)/shard_map/expand_conv/pallas_call | solution.py:491
  74.3 0.7 project_3.3
  75.0 3.9 %collective-permute-start.19 = (bf16[848,128]{1,0:T(8,128)(2,1)S(1)}, bf16[848,128]{1,0:T(8,128)(2,1)S(1)}, u32[]{:S(2)}, u32[]{:S(2)}) collective-permute-start(bf16[848,128]{1,0:T(8,128)(2,1)S(1)} %project_3.3), channel_id=1, source_target_pairs={{0,1},{3,2},{4,5},{7,6},{8,9},{11,10},{12,13},{15,14},{16,17},{19,... | collective-permute-start | bytes 651272 | tf_op jit(solution)/shard_map/ppermute | solution.py:524
  79.0 0.7 collective-permute-start.23
  79.7 0.7 project_0.2.share_ref
  80.3 1.3 %collective-permute-done.21.refs_1_ = bf16[1120,128]{1,0:T(8,128)(2,1)S(1)} collective-permute-done((bf16[1120,128]{1,0:T(8,128)(2,1)S(1)}, bf16[1120,128]{1,0:T(8,128)(2,1)S(1)}, u32[]{:S(2)}, u32[]{:S(2)}) %collective-permute-start.21) | collective-permute-done | bytes 286752 | tf_op jit(solution)/shard_map/ppermute | solution.py:534
  81.6 0.8 finish.2.refs_2_
  82.4 0.7 project_2.3
  83.1 2.5 %collective-permute-start.22 = (bf16[848,128]{1,0:T(8,128)(2,1)S(1)}, bf16[848,128]{1,0:T(8,128)(2,1)S(1)}, u32[]{:S(2)}, u32[]{:S(2)}) collective-permute-start(bf16[848,128]{1,0:T(8,128)(2,1)S(1)} %project_2.3), channel_id=1, source_target_pairs={{0,2},{1,3},{2,0},{3,1},{4,6},{5,7},{6,4},{7,5},{8,10},{9,11},{10,... | collective-permute-start | bytes 651272 | tf_op jit(solution)/shard_map/ppermute | solution.py:532
  85.6 0.7 project_1.3
  86.4 8.6 %collective-permute-done.22.unit_ref = bf16[848,128]{1,0:T(8,128)(2,1)S(1)} collective-permute-done((bf16[848,128]{1,0:T(8,128)(2,1)S(1)}, bf16[848,128]{1,0:T(8,128)(2,1)S(1)}, u32[]{:S(2)}, u32[]{:S(2)}) %collective-permute-start.22) | collective-permute-done | bytes 217120 | tf_op jit(solution)/shard_map/ppermute | solution.py:532
  95.0 0.6 project_0.3.share_ref
  95.7 1.7 %finish.3 = bf16[4,2,64,560]{3,2,1,0:T(8,128)(2,1)} custom-call(s32[4]{0:T(128)S(1)} %copy-done.5, f32[4,96,128]{2,1,0:T(8,128)S(1)} %get-tuple-element.33.refs_4_.refs_5_.mask_ref, f32[560,192]{1,0:T(8,128)S(1)} %project_0.3.share_ref, bf16[848,128]{1,0:T(8,128)(2,1)S(1)} %collective-permute-done.23.refs_0_, ...), custom_call_target="tpu_custom_call" | custom-call | flops 99999997952 | bytes 1000000000 | tf_op jit(solution)/shard_map/finish/pallas_call | solution.py:545
  (50 shorter events, 0.6 us)
Async XLA Ops:
  0.0 1.1 %copy-start = (bf16[4,2,64,560]{3,2,1,0:T(8,128)(2,1)S(1)}, bf16[4,2,64,560]{3,2,1,0:T(8,128)(2,1)}, u32[]{:S(2)}) copy-start(bf16[4,2,64,560]{3,2,1,0:T(8,128)(2,1)} %x_ref.1) | copy-start | bytes 1720324
  1.1 0.7 copy-start.4
  2.4 16.1 %collective-permute-start.3 = (bf16[2,144,512]{2,1,0:T(8,128)(2,1)S(1)}, bf16[2,144,512]{2,1,0:T(8,128)(2,1)S(1)}, u32[]{:S(2)}, u32[]{:S(2)}) collective-permute-start(bf16[2,144,512]{2,1,0:T(8,128)(2,1)S(1)} %get-tuple-element.35.refs_0_), channel_id=1, source_target_pairs={{0,2},{1,3},{2,0},{3,1},{4,6},{5,7},{6,4},{7,5},{8,10},{9,11},{10,... | collective-permute-start | bytes 884744 | tf_op jit(solution)/shard_map/ppermute | solution.py:425
  5.1 6.4 %collective-permute-start = (bf16[1,112,512]{2,1,0:T(8,128)(2,1)S(1)}, bf16[1,112,512]{2,1,0:T(8,128)(2,1)S(1)}, u32[]{:S(2)}, u32[]{:S(2)}) collective-permute-start(bf16[1,112,512]{2,1,0:T(8,128)(2,1)S(1)} %get-tuple-element.68), channel_id=1, source_target_pairs={{0,4},{4,0},{8,12},{12,8},{16,20},{20,16},{24,28},{28,24},{1,5},{5... | collective-permute-start | bytes 344072 | tf_op jit(solution)/shard_map/ppermute | solution.py:420
  5.2 13.3 %collective-permute-start.1 = (bf16[1,144,512]{2,1,0:T(8,128)(2,1)S(1)}, bf16[1,144,512]{2,1,0:T(8,128)(2,1)S(1)}, u32[]{:S(2)}, u32[]{:S(2)}) collective-permute-start(bf16[1,144,512]{2,1,0:T(8,128)(2,1)S(1)} %get-tuple-element.60), channel_id=1, source_target_pairs={{0,4},{4,0},{8,12},{12,8},{16,20},{20,16},{24,28},{28,24},{1,5},{5... | collective-permute-start | bytes 442376 | tf_op jit(solution)/shard_map/ppermute | solution.py:420
  5.7 12.8 %collective-permute-start.5 = (bf16[1,144,512]{2,1,0:T(8,128)(2,1)S(1)}, bf16[1,144,512]{2,1,0:T(8,128)(2,1)S(1)}, u32[]{:S(2)}, u32[]{:S(2)}) collective-permute-start(bf16[1,144,512]{2,1,0:T(8,128)(2,1)S(1)} %get-tuple-element.59), channel_id=1, source_target_pairs={{4,8},{12,16},{20,24},{8,4},{16,12},{24,20},{5,9},{13,17},{21,25},... | collective-permute-start | bytes 442376 | tf_op jit(solution)/shard_map/ppermute | solution.py:421
  7.8 20.7 %copy-start.1 = (f32[3,3,2,1400]{3,2,1,0:T(2,128)S(1)}, f32[3,3,2,1400]{3,2,1,0:T(2,128)}, u32[]{:S(2)}) copy-start(f32[3,3,2,1400]{3,2,1,0:T(2,128)} %dw_ref) | copy-start | bytes 302404
  7.8 20.7 %copy-start.2 = (f32[2,1400]{1,0:T(2,128)S(1)}, f32[2,1400]{1,0:T(2,128)}, u32[]{:S(2)}) copy-start(f32[2,1400]{1,0:T(2,128)} %eb_ref.1) | copy-start | bytes 33604
  7.8 20.7 %copy-start.3 = (f32[2,1400]{1,0:T(2,128)S(1)}, f32[2,1400]{1,0:T(2,128)}, u32[]{:S(2)}) copy-start(f32[2,1400]{1,0:T(2,128)} %db_ref.1) | copy-start | bytes 33604
  7.8 20.7 %copy-start.6 = (s32[4]{0:T(128)S(1)}, s32[4]{0:T(128)}, u32[]{:S(2)}) copy-start(s32[4]{0:T(128)} %height_ref.1) | copy-start | bytes 52
  7.9 10.6 %collective-permute-start.6 = (bf16[1,112,512]{2,1,0:T(8,128)(2,1)S(1)}, bf16[1,112,512]{2,1,0:T(8,128)(2,1)S(1)}, u32[]{:S(2)}, u32[]{:S(2)}) collective-permute-start(bf16[1,112,512]{2,1,0:T(8,128)(2,1)S(1)} %get-tuple-element.67), channel_id=1, source_target_pairs={{4,8},{12,16},{20,24},{8,4},{16,12},{24,20},{5,9},{13,17},{21,25},... | collective-permute-start | bytes 344072 | tf_op jit(solution)/shard_map/ppermute | solution.py:421
  11.5 13.3 %collective-permute-start.2 = (bf16[2,144,512]{2,1,0:T(8,128)(2,1)S(1)}, bf16[2,144,512]{2,1,0:T(8,128)(2,1)S(1)}, u32[]{:S(2)}, u32[]{:S(2)}) collective-permute-start(bf16[2,144,512]{2,1,0:T(8,128)(2,1)S(1)} %get-tuple-element.35.refs_0_), channel_id=1, source_target_pairs={{0,1},{1,0},{2,3},{3,2},{4,5},{5,4},{6,7},{7,6},{8,9},{9,8},{10,11... | collective-permute-start | bytes 884744 | tf_op jit(solution)/shard_map/ppermute | solution.py:426
  18.5 10.6 %collective-permute-start.7 = (bf16[2,144,512]{2,1,0:T(8,128)(2,1)S(1)}, bf16[2,144,512]{2,1,0:T(8,128)(2,1)S(1)}, u32[]{:S(2)}, u32[]{:S(2)}) collective-permute-start(bf16[2,144,512]{2,1,0:T(8,128)(2,1)S(1)} %get-tuple-element.35.refs_0_), channel_id=1, source_target_pairs={{1,2},{2,1},{5,6},{6,5},{9,10},{10,9},{13,14},{14,13},{17,18},{18,... | collective-permute-start | bytes 884744 | tf_op jit(solution)/shard_map/ppermute | solution.py:427
  19.2 11.9 %collective-permute-start.8 = (bf16[2,144,512]{2,1,0:T(8,128)(2,1)S(1)}, bf16[2,144,512]{2,1,0:T(8,128)(2,1)S(1)}, u32[]{:S(2)}, u32[]{:S(2)}) collective-permute-start(bf16[2,144,512]{2,1,0:T(8,128)(2,1)S(1)} %collective-permute-done.3.refs_2_), channel_id=1, source_target_pairs={{2,3},{1,0},{6,7},{5,4},{10,11},{9,8},{14,15},{13,12},{18,19},{17,... | collective-permute-start | bytes 884744 | tf_op jit(solution)/shard_map/ppermute | solution.py:428
  24.8 10.8 %collective-permute-start.10 = (bf16[2,144,512]{2,1,0:T(8,128)(2,1)S(1)}, bf16[2,144,512]{2,1,0:T(8,128)(2,1)S(1)}, u32[]{:S(2)}, u32[]{:S(2)}) collective-permute-start(bf16[2,144,512]{2,1,0:T(8,128)(2,1)S(1)} %pad_maximum_fusion.3), channel_id=1, source_target_pairs={{4,8},{12,16},{20,24},{8,4},{16,12},{24,20},{5,9},{13,17},{21,25},... | collective-permute-start | bytes 884744 | tf_op jit(solution)/shard_map/ppermute | solution.py:421
  26.8 10.8 %collective-permute-start.4 = (bf16[2,144,512]{2,1,0:T(8,128)(2,1)S(1)}, bf16[2,144,512]{2,1,0:T(8,128)(2,1)S(1)}, u32[]{:S(2)}, u32[]{:S(2)}) collective-permute-start(bf16[2,144,512]{2,1,0:T(8,128)(2,1)S(1)} %pad_maximum_fusion.2), channel_id=1, source_target_pairs={{0,4},{4,0},{8,12},{12,8},{16,20},{20,16},{24,28},{28,24},{1,5},{5... | collective-permute-start | bytes 884744 | tf_op jit(solution)/shard_map/ppermute | solution.py:420
  31.2 22.3 %collective-permute-start.14 = (bf16[2,112,512]{2,1,0:T(8,128)(2,1)S(1)}, bf16[2,112,512]{2,1,0:T(8,128)(2,1)S(1)}, u32[]{:S(2)}, u32[]{:S(2)}) collective-permute-start(bf16[2,112,512]{2,1,0:T(8,128)(2,1)S(1)} %get-tuple-element.48.refs_0_), channel_id=1, source_target_pairs={{0,1},{1,0},{2,3},{3,2},{4,5},{5,4},{6,7},{7,6},{8,9},{9,8},{10,11... | collective-permute-start | bytes 688136 | tf_op jit(solution)/shard_map/ppermute | solution.py:433
  31.3 22.2 %collective-permute-start.15 = (bf16[2,112,512]{2,1,0:T(8,128)(2,1)S(1)}, bf16[2,112,512]{2,1,0:T(8,128)(2,1)S(1)}, u32[]{:S(2)}, u32[]{:S(2)}) collective-permute-start(bf16[2,112,512]{2,1,0:T(8,128)(2,1)S(1)} %get-tuple-element.48.refs_0_), channel_id=1, source_target_pairs={{0,2},{1,3},{2,0},{3,1},{4,6},{5,7},{6,4},{7,5},{8,10},{9,11},{10,... | collective-permute-start | bytes 688136 | tf_op jit(solution)/shard_map/ppermute | solution.py:433
  35.3 18.2 %collective-permute-start.16 = (bf16[2,112,512]{2,1,0:T(8,128)(2,1)S(1)}, bf16[2,112,512]{2,1,0:T(8,128)(2,1)S(1)}, u32[]{:S(2)}, u32[]{:S(2)}) collective-permute-start(bf16[2,112,512]{2,1,0:T(8,128)(2,1)S(1)} %get-tuple-element.48.refs_0_), channel_id=1, source_target_pairs={{0,3},{1,2},{2,1},{3,0},{4,7},{5,6},{6,5},{7,4},{8,11},{9,10},{10,... | collective-permute-start | bytes 688136 | tf_op jit(solution)/shard_map/ppermute | solution.py:433
  35.6 8.0 %collective-permute-start.11 = (bf16[1,144,512]{2,1,0:T(8,128)(2,1)S(1)}, bf16[1,144,512]{2,1,0:T(8,128)(2,1)S(1)}, u32[]{:S(2)}, u32[]{:S(2)}) collective-permute-start(bf16[1,144,512]{2,1,0:T(8,128)(2,1)S(1)} %get-tuple-element.53), channel_id=1, source_target_pairs={{4,8},{12,16},{20,24},{8,4},{16,12},{24,20},{5,9},{13,17},{21,25},... | collective-permute-start | bytes 442376 | tf_op jit(solution)/shard_map/ppermute | solution.py:421
  37.6 6.1 %collective-permute-start.9 = (bf16[1,144,512]{2,1,0:T(8,128)(2,1)S(1)}, bf16[1,144,512]{2,1,0:T(8,128)(2,1)S(1)}, u32[]{:S(2)}, u32[]{:S(2)}) collective-permute-start(bf16[1,144,512]{2,1,0:T(8,128)(2,1)S(1)} %get-tuple-element.54), channel_id=1, source_target_pairs={{0,4},{4,0},{8,12},{12,8},{16,20},{20,16},{24,28},{28,24},{1,5},{5... | collective-permute-start | bytes 442376 | tf_op jit(solution)/shard_map/ppermute | solution.py:420
  39.6 10.9 %slice-start = ((s8[6307840]{0:T(1024)(128)(4,1)}), s8[4194304]{0:T(1024)(128)(4,1)S(1)}, s32[]{:S(2)}) async-start(s8[6307840]{0:T(1024)(128)(4,1)} %bitcast.1), calls=%async_computation | async-start | bytes 8388608
  43.6 6.9 %slice-start.1 = ((s8[6307840]{0:T(1024)(128)(4,1)}), s8[2113536]{0:T(1024)(128)(4,1)S(1)}, s32[]{:S(2)}) async-start(s8[6307840]{0:T(1024)(128)(4,1)} %bitcast.1), calls=%async_computation.1 | async-start | bytes 4227072
  51.1 8.4 %collective-permute-start.12 = (bf16[1120,128]{1,0:T(8,128)(2,1)S(1)}, bf16[1120,128]{1,0:T(8,128)(2,1)S(1)}, u32[]{:S(2)}, u32[]{:S(2)}) collective-permute-start(bf16[1120,128]{1,0:T(8,128)(2,1)S(1)} %project_3.2), channel_id=1, source_target_pairs={{0,1},{3,2},{4,5},{7,6},{8,9},{11,10},{12,13},{15,14},{16,17},{19,... | collective-permute-start | bytes 860168 | tf_op jit(solution)/shard_map/ppermute | solution.py:524
  52.8 6.8 %collective-permute-start.13 = (bf16[1120,128]{1,0:T(8,128)(2,1)S(1)}, bf16[1120,128]{1,0:T(8,128)(2,1)S(1)}, u32[]{:S(2)}, u32[]{:S(2)}) collective-permute-start(bf16[1120,128]{1,0:T(8,128)(2,1)S(1)} %project_3.2), channel_id=1, source_target_pairs={{1,2},{2,1},{5,6},{6,5},{9,10},{10,9},{13,14},{14,13},{17,18},{18,... | collective-permute-start | bytes 860168 | tf_op jit(solution)/shard_map/ppermute | solution.py:525
  53.6 15.6 %collective-permute-start.18 = (bf16[3,112,512]{2,1,0:T(8,128)(2,1)S(1)}, bf16[3,112,512]{2,1,0:T(8,128)(2,1)S(1)}, u32[]{:S(2)}, u32[]{:S(2)}) collective-permute-start(bf16[3,112,512]{2,1,0:T(8,128)(2,1)S(1)} %pad_maximum_fusion.1), channel_id=1, source_target_pairs={{4,8},{12,16},{20,24},{8,4},{16,12},{24,20},{5,9},{13,17},{21,25},... | collective-permute-start | bytes 1032200 | tf_op jit(solution)/shard_map/ppermute | solution.py:421
  55.8 13.4 %collective-permute-start.17 = (bf16[3,112,512]{2,1,0:T(8,128)(2,1)S(1)}, bf16[3,112,512]{2,1,0:T(8,128)(2,1)S(1)}, u32[]{:S(2)}, u32[]{:S(2)}) collective-permute-start(bf16[3,112,512]{2,1,0:T(8,128)(2,1)S(1)} %pad_maximum_fusion), channel_id=1, source_target_pairs={{0,4},{4,0},{8,12},{12,8},{16,20},{20,16},{24,28},{28,24},{1,5},{5... | collective-permute-start | bytes 1032200 | tf_op jit(solution)/shard_map/ppermute | solution.py:420
  60.2 19.5 %collective-permute-start.20 = (bf16[1120,128]{1,0:T(8,128)(2,1)S(1)}, bf16[1120,128]{1,0:T(8,128)(2,1)S(1)}, u32[]{:S(2)}, u32[]{:S(2)}) collective-permute-start(bf16[1120,128]{1,0:T(8,128)(2,1)S(1)} %project_2.2), channel_id=1, source_target_pairs={{0,2},{1,3},{2,0},{3,1},{4,6},{5,7},{6,4},{7,5},{8,10},{9,11},{10,... | collective-permute-start | bytes 860168 | tf_op jit(solution)/shard_map/ppermute | solution.py:532
  69.1 12.5 %collective-permute-start.21 = (bf16[1120,128]{1,0:T(8,128)(2,1)S(1)}, bf16[1120,128]{1,0:T(8,128)(2,1)S(1)}, u32[]{:S(2)}, u32[]{:S(2)}) collective-permute-start(bf16[1120,128]{1,0:T(8,128)(2,1)S(1)} %project_1.2), channel_id=1, source_target_pairs={{0,1},{1,0},{2,3},{3,2},{4,5},{5,4},{6,7},{7,6},{8,9},{9,8},{10,11... | collective-permute-start | bytes 860168 | tf_op jit(solution)/shard_map/ppermute | solution.py:534
  75.0 6.6 %copy-start.5 = (s32[4]{0:T(128)S(1)}, s32[4]{0:T(128)}, u32[]{:S(2)}) copy-start(s32[4]{0:T(128)} %width_ref.7) | copy-start | bytes 52
  75.0 7.4 %collective-permute-start.19 = (bf16[848,128]{1,0:T(8,128)(2,1)S(1)}, bf16[848,128]{1,0:T(8,128)(2,1)S(1)}, u32[]{:S(2)}, u32[]{:S(2)}) collective-permute-start(bf16[848,128]{1,0:T(8,128)(2,1)S(1)} %project_3.3), channel_id=1, source_target_pairs={{0,1},{3,2},{4,5},{7,6},{8,9},{11,10},{12,13},{15,14},{16,17},{19,... | collective-permute-start | bytes 651272 | tf_op jit(solution)/shard_map/ppermute | solution.py:524
  79.0 7.3 %collective-permute-start.23 = (bf16[848,128]{1,0:T(8,128)(2,1)S(1)}, bf16[848,128]{1,0:T(8,128)(2,1)S(1)}, u32[]{:S(2)}, u32[]{:S(2)}) collective-permute-start(bf16[848,128]{1,0:T(8,128)(2,1)S(1)} %project_3.3), channel_id=1, source_target_pairs={{1,2},{2,1},{5,6},{6,5},{9,10},{10,9},{13,14},{14,13},{17,18},{18,... | collective-permute-start | bytes 651272 | tf_op jit(solution)/shard_map/ppermute | solution.py:525
  83.1 11.9 %collective-permute-start.22 = (bf16[848,128]{1,0:T(8,128)(2,1)S(1)}, bf16[848,128]{1,0:T(8,128)(2,1)S(1)}, u32[]{:S(2)}, u32[]{:S(2)}) collective-permute-start(bf16[848,128]{1,0:T(8,128)(2,1)S(1)} %project_2.3), channel_id=1, source_target_pairs={{0,2},{1,3},{2,0},{3,1},{4,6},{5,7},{6,4},{7,5},{8,10},{9,11},{10,... | collective-permute-start | bytes 651272 | tf_op jit(solution)/shard_map/ppermute | solution.py:532
  86.3 9.3 %collective-permute-start.24 = (bf16[848,128]{1,0:T(8,128)(2,1)S(1)}, bf16[848,128]{1,0:T(8,128)(2,1)S(1)}, u32[]{:S(2)}, u32[]{:S(2)}) collective-permute-start(bf16[848,128]{1,0:T(8,128)(2,1)S(1)} %project_1.3), channel_id=1, source_target_pairs={{0,1},{1,0},{2,3},{3,2},{4,5},{5,4},{6,7},{7,6},{8,9},{9,8},{10,11... | collective-permute-start | bytes 651272 | tf_op jit(solution)/shard_map/ppermute | solution.py:534

commit v3 on v2

--- a/solution.py
+++ b/solution.py
@@ -424,8 +424,8 @@
     def relay(mine, tables, *others):
         second = lax.ppermute(mine, "tensor", two_off)
         first = lax.ppermute(mine, "tensor", near)
-        across = lax.ppermute(after(mine, second, *others), "tensor", middle)
-        passed = lax.ppermute(after(second, *others), "tensor", to_end)
+        across = lax.ppermute(after(mine, second, first, *others), "tensor", middle)
+        passed = lax.ppermute(after(second, first, *others), "tensor", to_end)
         return [mine, first, second, after(across, tables) + passed]
 
     def direct(mine):

time: 98.7 us -> 98.2 us (level)
  waiting for transfers between devices: 17.6 us -> 18.9 us
    ppermute x1, waiting for transfers between devices: 4.2 us -> 0.01 us  [relay(): first = lax.ppermute(mine, 'tensor', near)]
    ppermute x2, waiting for transfers between devices: 1.88 us -> 4.77 us  [the longest x1 4.76 us: relay(): passed = lax.ppermute(after(second, first, *others), 'tensor', to_end)]
    ppermute x5, starting transfers between devices: 6.6 us -> 4.51 us  [send_rows(): lax.ppermute(x, 'row', sibling)]
    ppermute x2, waiting for transfers between devices: 1.55 us -> 3.15 us  [on_device_packed(): relayed = lax.ppermute(far, 'tensor', from_end)]
    ppermute x2, starting transfers between devices: 5.54 us -> 6.98 us  [on_device_packed(): relayed = lax.ppermute(far, 'tensor', from_end)]
    ppermute x1, waiting for transfers between devices: 0.03 us -> 1.31 us  [relay(): second = lax.ppermute(mine, 'tensor', two_off)]
  transfers between devices with their start and end apart: 25 -> 25, of which waited for: 5 -> 7; matrix products, arithmetic and copies ran while one was open for 0% -> 0% of each run, Pallas kernels for 32% -> 32%
where the time goes in v3:
time: 98.2 us; the launch traced here: 97.8 us
  starting transfers between devices  42.8 us (44%)
  Pallas kernels  33.4 us (34%)
  waiting for transfers between devices  18.9 us (19%)
  local copies, waits for them, and re-layouts  1.94 us (2%)
    pallas_call x2, Pallas kernels, on_device_packed(): pl.pallas_call(functools.partial(hidden_kernel, chunk=chunk, shards=shard...  12 us
    ppermute x5, starting transfers between devices, send_rows(): lax.ppermute(x, 'row', beyond)  11.6 us
    ppermute x2, waiting for transfers between devices, on_device_packed(): distant = lax.ppermute(last_unit, 'tensor', two_off)  8.03 us
    ppermute x2, starting transfers between devices, on_device_packed(): distant = lax.ppermute(last_unit, 'tensor', two_off)  7.56 us
    pallas_call x2, Pallas kernels, on_device_packed(): pl.pallas_call(functools.partial(own_kernel, chunk=chunk, shards=shards),...  7.06 us
    ppermute x2, starting transfers between devices, on_device_packed(): relayed = lax.ppermute(far, 'tensor', from_end)  6.98 us
    pallas_call x1, Pallas kernels, on_device_packed(): pl.pallas_call(functools.partial(load_kernel, shards=shards, depth=depth)...  5.34 us
    ppermute x1, waiting for transfers between devices, relay(): passed = lax.ppermute(after(second, first, *others), 'tensor', to_end)  4.76 us
  transfers between devices with their start and end apart: 25, of which 7 were waited for; matrix products, arithmetic and copies ran while one was open for 0% of the time, Pallas kernels for 32%

profile of v3, /device:TPU:2, one launch (start us, length us, event | category | flops | bytes accessed | tf_op | source)
XLA Modules:
  0.0 97.8 jit_solution(15609374672580420088)
XLA Ops:
  0.0 1.1 %copy-done = bf16[4,2,64,560]{3,2,1,0:T(8,128)(2,1)S(1)} copy-done((bf16[4,2,64,560]{3,2,1,0:T(8,128)(2,1)S(1)}, bf16[4,2,64,560]{3,2,1,0:T(8,128)(2,1)}, u32[]{:S(2)}) %copy-start) | copy-done | bytes 573464
  1.1 0.7 copy-done.4
  1.7 0.7 pack.1
  2.4 1.6 %collective-permute-start.2 = (bf16[2,144,512]{2,1,0:T(8,128)(2,1)S(1)}, bf16[2,144,512]{2,1,0:T(8,128)(2,1)S(1)}, u32[]{:S(2)}, u32[]{:S(2)}) collective-permute-start(bf16[2,144,512]{2,1,0:T(8,128)(2,1)S(1)} %get-tuple-element.35.refs_0_), channel_id=1, source_target_pairs={{0,1},{1,0},{2,3},{3,2},{4,5},{5,4},{6,7},{7,6},{8,9},{9,8},{10,11... | collective-permute-start | bytes 884744 | tf_op jit(solution)/shard_map/ppermute | solution.py:426
  4.0 2.6 %collective-permute-start.3 = (bf16[2,144,512]{2,1,0:T(8,128)(2,1)S(1)}, bf16[2,144,512]{2,1,0:T(8,128)(2,1)S(1)}, u32[]{:S(2)}, u32[]{:S(2)}) collective-permute-start(bf16[2,144,512]{2,1,0:T(8,128)(2,1)S(1)} %get-tuple-element.35.refs_0_), channel_id=1, source_target_pairs={{0,2},{1,3},{2,0},{3,1},{4,6},{5,7},{6,4},{7,5},{8,10},{9,11},{10,... | collective-permute-start | bytes 884744 | tf_op jit(solution)/shard_map/ppermute | solution.py:425
  6.8 0.6 collective-permute-start.1
  7.3 2.1 %collective-permute-start.5 = (bf16[1,144,512]{2,1,0:T(8,128)(2,1)S(1)}, bf16[1,144,512]{2,1,0:T(8,128)(2,1)S(1)}, u32[]{:S(2)}, u32[]{:S(2)}) collective-permute-start(bf16[1,144,512]{2,1,0:T(8,128)(2,1)S(1)} %get-tuple-element.59), channel_id=1, source_target_pairs={{4,8},{12,16},{20,24},{8,4},{16,12},{24,20},{5,9},{13,17},{21,25},... | collective-permute-start | bytes 442376 | tf_op jit(solution)/shard_map/ppermute | solution.py:421
  9.4 3.6 %collective-permute-start.6 = (bf16[1,112,512]{2,1,0:T(8,128)(2,1)S(1)}, bf16[1,112,512]{2,1,0:T(8,128)(2,1)S(1)}, u32[]{:S(2)}, u32[]{:S(2)}) collective-permute-start(bf16[1,112,512]{2,1,0:T(8,128)(2,1)S(1)} %get-tuple-element.67), channel_id=1, source_target_pairs={{4,8},{12,16},{20,24},{8,4},{16,12},{24,20},{5,9},{13,17},{21,25},... | collective-permute-start | bytes 344072 | tf_op jit(solution)/shard_map/ppermute | solution.py:421
  13.1 5.3 %load_weights.1 = (bf16[2,2240,1400]{2,1,0:T(8,128)(2,1)S(1)}, f32[8,128]{1,0:T(8,128)}) custom-call(bf16[2,2240,1400]{2,1,0:T(8,128)(2,1)} %w_ref), custom_call_target="tpu_custom_call" | custom-call | tf_op jit(solution)/shard_map/load_weights/pallas_call | solution.py:438
  18.5 1.3 %collective-permute-done.3.refs_2_ = bf16[2,144,512]{2,1,0:T(8,128)(2,1)S(1)} collective-permute-done((bf16[2,144,512]{2,1,0:T(8,128)(2,1)S(1)}, bf16[2,144,512]{2,1,0:T(8,128)(2,1)S(1)}, u32[]{:S(2)}, u32[]{:S(2)}) %collective-permute-start.3) | collective-permute-done | bytes 294944 | tf_op jit(solution)/shard_map/ppermute | solution.py:425
  19.8 0.7 collective-permute-start.7
  20.5 1.3 %collective-permute-start.8 = (bf16[2,144,512]{2,1,0:T(8,128)(2,1)S(1)}, bf16[2,144,512]{2,1,0:T(8,128)(2,1)S(1)}, u32[]{:S(2)}, u32[]{:S(2)}) collective-permute-start(bf16[2,144,512]{2,1,0:T(8,128)(2,1)S(1)} %collective-permute-done.3.refs_2_), channel_id=1, source_target_pairs={{2,3},{1,0},{6,7},{5,4},{10,11},{9,8},{14,15},{13,12},{18,19},{17,... | collective-permute-start | bytes 884744 | tf_op jit(solution)/shard_map/ppermute | solution.py:428
  21.9 1.9 %collective-permute-start.10 = (bf16[2,144,512]{2,1,0:T(8,128)(2,1)S(1)}, bf16[2,144,512]{2,1,0:T(8,128)(2,1)S(1)}, u32[]{:S(2)}, u32[]{:S(2)}) collective-permute-start(bf16[2,144,512]{2,1,0:T(8,128)(2,1)S(1)} %pad_maximum_fusion.3), channel_id=1, source_target_pairs={{4,8},{12,16},{20,24},{8,4},{16,12},{24,20},{5,9},{13,17},{21,25},... | collective-permute-start | bytes 884744 | tf_op jit(solution)/shard_map/ppermute | solution.py:421
  23.8 1.7 %collective-permute-start.4 = (bf16[2,144,512]{2,1,0:T(8,128)(2,1)S(1)}, bf16[2,144,512]{2,1,0:T(8,128)(2,1)S(1)}, u32[]{:S(2)}, u32[]{:S(2)}) collective-permute-start(bf16[2,144,512]{2,1,0:T(8,128)(2,1)S(1)} %pad_maximum_fusion.2), channel_id=1, source_target_pairs={{0,4},{4,0},{8,12},{12,8},{16,20},{20,16},{24,28},{28,24},{1,5},{5... | collective-permute-start | bytes 884744 | tf_op jit(solution)/shard_map/ppermute | solution.py:420
  25.5 0.6 tables.1
  26.1 4.8 %collective-permute-done.8 = bf16[2,144,512]{2,1,0:T(8,128)(2,1)S(1)} collective-permute-done((bf16[2,144,512]{2,1,0:T(8,128)(2,1)S(1)}, bf16[2,144,512]{2,1,0:T(8,128)(2,1)S(1)}, u32[]{:S(2)}, u32[]{:S(2)}) %collective-permute-start.8) | collective-permute-done | bytes 294944 | tf_op jit(solution)/shard_map/ppermute | solution.py:428
  30.9 0.1 add.3.refs_3_
  31.1 2.5 %collective-permute-start.15 = (bf16[2,112,512]{2,1,0:T(8,128)(2,1)S(1)}, bf16[2,112,512]{2,1,0:T(8,128)(2,1)S(1)}, u32[]{:S(2)}, u32[]{:S(2)}) collective-permute-start(bf16[2,112,512]{2,1,0:T(8,128)(2,1)S(1)} %get-tuple-element.48.refs_0_), channel_id=1, source_target_pairs={{0,2},{1,3},{2,0},{3,1},{4,6},{5,7},{6,4},{7,5},{8,10},{9,11},{10,... | collective-permute-start | bytes 688136 | tf_op jit(solution)/shard_map/ppermute | solution.py:433
  33.6 1.9 %collective-permute-start.16 = (bf16[2,112,512]{2,1,0:T(8,128)(2,1)S(1)}, bf16[2,112,512]{2,1,0:T(8,128)(2,1)S(1)}, u32[]{:S(2)}, u32[]{:S(2)}) collective-permute-start(bf16[2,112,512]{2,1,0:T(8,128)(2,1)S(1)} %get-tuple-element.48.refs_0_), channel_id=1, source_target_pairs={{0,3},{1,2},{2,1},{3,0},{4,7},{5,6},{6,5},{7,4},{8,11},{9,10},{10,... | collective-permute-start | bytes 688136 | tf_op jit(solution)/shard_map/ppermute | solution.py:433
  35.5 1.9 %collective-permute-start.11 = (bf16[1,144,512]{2,1,0:T(8,128)(2,1)S(1)}, bf16[1,144,512]{2,1,0:T(8,128)(2,1)S(1)}, u32[]{:S(2)}, u32[]{:S(2)}) collective-permute-start(bf16[1,144,512]{2,1,0:T(8,128)(2,1)S(1)} %get-tuple-element.53), channel_id=1, source_target_pairs={{4,8},{12,16},{20,24},{8,4},{16,12},{24,20},{5,9},{13,17},{21,25},... | collective-permute-start | bytes 442376 | tf_op jit(solution)/shard_map/ppermute | solution.py:421
  37.4 0.8 collective-permute-start.9
  38.2 4.0 %expand_own.2.refs_6_ = f32[2,256,1400]{2,1,0:T(8,128)S(1)} custom-call(bf16[2,144,512]{2,1,0:T(8,128)(2,1)S(1)} %get-tuple-element.35.refs_0_, bf16[2,144,512]{2,1,0:T(8,128)(2,1)S(1)} %collective-permute-done.2.refs_1_, bf16[2,144,512]{2,1,0:T(8,128)(2,1)S(1)} %collective-permute-done.3.refs_2_, bf16[2,144,512]{2,1,0:T(8,128)(2,1)S(1)} %add.3.refs_3_, ...), custom_call_target="tpu_custom_call" | custom-call | flops 1000 | bytes 1000 | tf_op jit(solution)/shard_map/expand_own/pallas_call | solution.py:475
  42.2 6.8 %expand_conv.2.hidden_ref = bf16[256,1400]{1,0:T(8,128)(2,1)S(1)} custom-call(bf16[1,144,512]{2,1,0:T(8,128)(2,1)S(1)} %collective-permute-done.1.refs_0_, bf16[2,144,512]{2,1,0:T(8,128)(2,1)S(1)} %collective-permute-done.4.refs_1_, bf16[1,144,512]{2,1,0:T(8,128)(2,1)S(1)} %collective-permute-done.9.refs_2_, ...), custom_call_target="tpu_custom_call" | custom-call | flops 1000 | bytes 1000 | tf_op jit(solution)/shard_map/expand_conv/pallas_call | solution.py:491
  49.0 0.7 project_3.2
  49.7 3.1 %collective-permute-start.12 = (bf16[1120,128]{1,0:T(8,128)(2,1)S(1)}, bf16[1120,128]{1,0:T(8,128)(2,1)S(1)}, u32[]{:S(2)}, u32[]{:S(2)}) collective-permute-start(bf16[1120,128]{1,0:T(8,128)(2,1)S(1)} %project_3.2), channel_id=1, source_target_pairs={{0,1},{3,2},{4,5},{7,6},{8,9},{11,10},{12,13},{15,14},{16,17},{19,... | collective-permute-start | bytes 860168 | tf_op jit(solution)/shard_map/ppermute | solution.py:524
  52.8 0.7 collective-permute-start.13
  53.6 2.1 %collective-permute-start.18 = (bf16[3,112,512]{2,1,0:T(8,128)(2,1)S(1)}, bf16[3,112,512]{2,1,0:T(8,128)(2,1)S(1)}, u32[]{:S(2)}, u32[]{:S(2)}) collective-permute-start(bf16[3,112,512]{2,1,0:T(8,128)(2,1)S(1)} %pad_maximum_fusion.1), channel_id=1, source_target_pairs={{4,8},{12,16},{20,24},{8,4},{16,12},{24,20},{5,9},{13,17},{21,25},... | collective-permute-start | bytes 1032200 | tf_op jit(solution)/shard_map/ppermute | solution.py:421
  55.8 1.5 %collective-permute-start.17 = (bf16[3,112,512]{2,1,0:T(8,128)(2,1)S(1)}, bf16[3,112,512]{2,1,0:T(8,128)(2,1)S(1)}, u32[]{:S(2)}, u32[]{:S(2)}) collective-permute-start(bf16[3,112,512]{2,1,0:T(8,128)(2,1)S(1)} %pad_maximum_fusion), channel_id=1, source_target_pairs={{0,4},{4,0},{8,12},{12,8},{16,20},{20,16},{24,28},{28,24},{1,5},{5... | collective-permute-start | bytes 1032200 | tf_op jit(solution)/shard_map/ppermute | solution.py:420
  57.2 2.7 %collective-permute-done.12.refs_0_ = bf16[1120,128]{1,0:T(8,128)(2,1)S(1)} collective-permute-done((bf16[1120,128]{1,0:T(8,128)(2,1)S(1)}, bf16[1120,128]{1,0:T(8,128)(2,1)S(1)}, u32[]{:S(2)}, u32[]{:S(2)}) %collective-permute-start.12) | collective-permute-done | bytes 286752 | tf_op jit(solution)/shard_map/ppermute | solution.py:524
  60.0 0.6 project_2.2
  60.6 4.4 %collective-permute-start.20 = (bf16[1120,128]{1,0:T(8,128)(2,1)S(1)}, bf16[1120,128]{1,0:T(8,128)(2,1)S(1)}, u32[]{:S(2)}, u32[]{:S(2)}) collective-permute-start(bf16[1120,128]{1,0:T(8,128)(2,1)S(1)} %project_2.2), channel_id=1, source_target_pairs={{0,2},{1,3},{2,0},{3,1},{4,6},{5,7},{6,4},{7,5},{8,10},{9,11},{10,... | collective-permute-start | bytes 860168 | tf_op jit(solution)/shard_map/ppermute | solution.py:532
  65.1 0.6 project_1.2
  65.7 3.1 %expand_own.3.refs_4_ = f32[2,192,1400]{2,1,0:T(8,128)S(1)} custom-call(bf16[2,112,512]{2,1,0:T(8,128)(2,1)S(1)} %get-tuple-element.48.refs_0_, bf16[2,112,512]{2,1,0:T(8,128)(2,1)S(1)} %collective-permute-done.14.refs_1_, bf16[2,112,512]{2,1,0:T(8,128)(2,1)S(1)} %collective-permute-done.15.refs_2_, ...), custom_call_target="tpu_custom_call" | custom-call | flops 1000 | bytes 1000 | tf_op jit(solution)/shard_map/expand_own/pallas_call | solution.py:475
  68.9 5.1 %expand_conv.3.hidden_ref = bf16[192,1400]{1,0:T(8,128)(2,1)S(1)} custom-call(bf16[1,112,512]{2,1,0:T(8,128)(2,1)S(1)} %collective-permute-done.refs_0_, bf16[3,112,512]{2,1,0:T(8,128)(2,1)S(1)} %collective-permute-done.17.refs_1_, bf16[1,112,512]{2,1,0:T(8,128)(2,1)S(1)} %collective-permute-done.6.refs_2_, ...), custom_call_target="tpu_custom_call" | custom-call | flops 1000 | bytes 1000 | tf_op jit(solution)/shard_map/expand_conv/pallas_call | solution.py:491
  74.0 0.7 project_3.3
  74.7 3.9 %collective-permute-start.19 = (bf16[848,128]{1,0:T(8,128)(2,1)S(1)}, bf16[848,128]{1,0:T(8,128)(2,1)S(1)}, u32[]{:S(2)}, u32[]{:S(2)}) collective-permute-start(bf16[848,128]{1,0:T(8,128)(2,1)S(1)} %project_3.3), channel_id=1, source_target_pairs={{0,1},{3,2},{4,5},{7,6},{8,9},{11,10},{12,13},{15,14},{16,17},{19,... | collective-permute-start | bytes 651272 | tf_op jit(solution)/shard_map/ppermute | solution.py:524
  78.7 0.7 collective-permute-start.23
  79.3 0.7 project_0.2.share_ref
  80.0 1.4 %collective-permute-done.21.refs_1_ = bf16[1120,128]{1,0:T(8,128)(2,1)S(1)} collective-permute-done((bf16[1120,128]{1,0:T(8,128)(2,1)S(1)}, bf16[1120,128]{1,0:T(8,128)(2,1)S(1)}, u32[]{:S(2)}, u32[]{:S(2)}) %collective-permute-start.21) | collective-permute-done | bytes 286752 | tf_op jit(solution)/shard_map/ppermute | solution.py:534
  81.4 0.8 finish.2.refs_2_
  82.2 0.4 collective-permute-done.19.refs_0_
  82.6 0.7 project_2.3
  83.3 3.1 %collective-permute-start.22 = (bf16[848,128]{1,0:T(8,128)(2,1)S(1)}, bf16[848,128]{1,0:T(8,128)(2,1)S(1)}, u32[]{:S(2)}, u32[]{:S(2)}) collective-permute-start(bf16[848,128]{1,0:T(8,128)(2,1)S(1)} %project_2.3), channel_id=1, source_target_pairs={{0,2},{1,3},{2,0},{3,1},{4,6},{5,7},{6,4},{7,5},{8,10},{9,11},{10,... | collective-permute-start | bytes 651272 | tf_op jit(solution)/shard_map/ppermute | solution.py:532
  86.4 0.7 project_1.3
  87.2 8.0 %collective-permute-done.22.unit_ref = bf16[848,128]{1,0:T(8,128)(2,1)S(1)} collective-permute-done((bf16[848,128]{1,0:T(8,128)(2,1)S(1)}, bf16[848,128]{1,0:T(8,128)(2,1)S(1)}, u32[]{:S(2)}, u32[]{:S(2)}) %collective-permute-start.22) | collective-permute-done | bytes 217120 | tf_op jit(solution)/shard_map/ppermute | solution.py:532
  95.3 0.6 project_0.3.share_ref
  95.9 0.2 collective-permute-done.24.refs_1_
  96.1 1.7 %finish.3 = bf16[4,2,64,560]{3,2,1,0:T(8,128)(2,1)} custom-call(s32[4]{0:T(128)S(1)} %copy-done.5, f32[4,96,128]{2,1,0:T(8,128)S(1)} %get-tuple-element.33.refs_4_.refs_5_.mask_ref, f32[560,192]{1,0:T(8,128)S(1)} %project_0.3.share_ref, bf16[848,128]{1,0:T(8,128)(2,1)S(1)} %collective-permute-done.23.refs_0_, ...), custom_call_target="tpu_custom_call" | custom-call | flops 99999997952 | bytes 1000000000 | tf_op jit(solution)/shard_map/finish/pallas_call | solution.py:545
  (50 shorter events, 0.7 us)
Async XLA Ops:
  0.0 1.1 %copy-start = (bf16[4,2,64,560]{3,2,1,0:T(8,128)(2,1)S(1)}, bf16[4,2,64,560]{3,2,1,0:T(8,128)(2,1)}, u32[]{:S(2)}) copy-start(bf16[4,2,64,560]{3,2,1,0:T(8,128)(2,1)} %x_ref.1) | copy-start | bytes 1720324
  1.1 0.7 copy-start.4
  2.4 16.1 %collective-permute-start.2 = (bf16[2,144,512]{2,1,0:T(8,128)(2,1)S(1)}, bf16[2,144,512]{2,1,0:T(8,128)(2,1)S(1)}, u32[]{:S(2)}, u32[]{:S(2)}) collective-permute-start(bf16[2,144,512]{2,1,0:T(8,128)(2,1)S(1)} %get-tuple-element.35.refs_0_), channel_id=1, source_target_pairs={{0,1},{1,0},{2,3},{3,2},{4,5},{5,4},{6,7},{7,6},{8,9},{9,8},{10,11... | collective-permute-start | bytes 884744 | tf_op jit(solution)/shard_map/ppermute | solution.py:426
  4.0 15.7 %collective-permute-start.3 = (bf16[2,144,512]{2,1,0:T(8,128)(2,1)S(1)}, bf16[2,144,512]{2,1,0:T(8,128)(2,1)S(1)}, u32[]{:S(2)}, u32[]{:S(2)}) collective-permute-start(bf16[2,144,512]{2,1,0:T(8,128)(2,1)S(1)} %get-tuple-element.35.refs_0_), channel_id=1, source_target_pairs={{0,2},{1,3},{2,0},{3,1},{4,6},{5,7},{6,4},{7,5},{8,10},{9,11},{10,... | collective-permute-start | bytes 884744 | tf_op jit(solution)/shard_map/ppermute | solution.py:425
  6.7 2.7 %collective-permute-start = (bf16[1,112,512]{2,1,0:T(8,128)(2,1)S(1)}, bf16[1,112,512]{2,1,0:T(8,128)(2,1)S(1)}, u32[]{:S(2)}, u32[]{:S(2)}) collective-permute-start(bf16[1,112,512]{2,1,0:T(8,128)(2,1)S(1)} %get-tuple-element.68), channel_id=1, source_target_pairs={{0,4},{4,0},{8,12},{12,8},{16,20},{20,16},{24,28},{28,24},{1,5},{5... | collective-permute-start | bytes 344072 | tf_op jit(solution)/shard_map/ppermute | solution.py:420
  6.8 11.7 %collective-permute-start.1 = (bf16[1,144,512]{2,1,0:T(8,128)(2,1)S(1)}, bf16[1,144,512]{2,1,0:T(8,128)(2,1)S(1)}, u32[]{:S(2)}, u32[]{:S(2)}) collective-permute-start(bf16[1,144,512]{2,1,0:T(8,128)(2,1)S(1)} %get-tuple-element.60), channel_id=1, source_target_pairs={{0,4},{4,0},{8,12},{12,8},{16,20},{20,16},{24,28},{28,24},{1,5},{5... | collective-permute-start | bytes 442376 | tf_op jit(solution)/shard_map/ppermute | solution.py:420
  7.3 11.1 %collective-permute-start.5 = (bf16[1,144,512]{2,1,0:T(8,128)(2,1)S(1)}, bf16[1,144,512]{2,1,0:T(8,128)(2,1)S(1)}, u32[]{:S(2)}, u32[]{:S(2)}) collective-permute-start(bf16[1,144,512]{2,1,0:T(8,128)(2,1)S(1)} %get-tuple-element.59), channel_id=1, source_target_pairs={{4,8},{12,16},{20,24},{8,4},{16,12},{24,20},{5,9},{13,17},{21,25},... | collective-permute-start | bytes 442376 | tf_op jit(solution)/shard_map/ppermute | solution.py:421
  9.4 16.1 %copy-start.1 = (f32[3,3,2,1400]{3,2,1,0:T(2,128)S(1)}, f32[3,3,2,1400]{3,2,1,0:T(2,128)}, u32[]{:S(2)}) copy-start(f32[3,3,2,1400]{3,2,1,0:T(2,128)} %dw_ref) | copy-start | bytes 302404
  9.4 16.1 %copy-start.2 = (f32[2,1400]{1,0:T(2,128)S(1)}, f32[2,1400]{1,0:T(2,128)}, u32[]{:S(2)}) copy-start(f32[2,1400]{1,0:T(2,128)} %eb_ref.1) | copy-start | bytes 33604
  9.4 16.1 %copy-start.3 = (f32[2,1400]{1,0:T(2,128)S(1)}, f32[2,1400]{1,0:T(2,128)}, u32[]{:S(2)}) copy-start(f32[2,1400]{1,0:T(2,128)} %db_ref.1) | copy-start | bytes 33604
  9.4 16.1 %copy-start.6 = (s32[4]{0:T(128)S(1)}, s32[4]{0:T(128)}, u32[]{:S(2)}) copy-start(s32[4]{0:T(128)} %height_ref.1) | copy-start | bytes 52
  9.4 9.0 %collective-permute-start.6 = (bf16[1,112,512]{2,1,0:T(8,128)(2,1)S(1)}, bf16[1,112,512]{2,1,0:T(8,128)(2,1)S(1)}, u32[]{:S(2)}, u32[]{:S(2)}) collective-permute-start(bf16[1,112,512]{2,1,0:T(8,128)(2,1)S(1)} %get-tuple-element.67), channel_id=1, source_target_pairs={{4,8},{12,16},{20,24},{8,4},{16,12},{24,20},{5,9},{13,17},{21,25},... | collective-permute-start | bytes 344072 | tf_op jit(solution)/shard_map/ppermute | solution.py:421
  19.8 6.3 %collective-permute-start.7 = (bf16[2,144,512]{2,1,0:T(8,128)(2,1)S(1)}, bf16[2,144,512]{2,1,0:T(8,128)(2,1)S(1)}, u32[]{:S(2)}, u32[]{:S(2)}) collective-permute-start(bf16[2,144,512]{2,1,0:T(8,128)(2,1)S(1)} %get-tuple-element.35.refs_0_), channel_id=1, source_target_pairs={{1,2},{2,1},{5,6},{6,5},{9,10},{10,9},{13,14},{14,13},{17,18},{18,... | collective-permute-start | bytes 884744 | tf_op jit(solution)/shard_map/ppermute | solution.py:427
  20.5 10.4 %collective-permute-start.8 = (bf16[2,144,512]{2,1,0:T(8,128)(2,1)S(1)}, bf16[2,144,512]{2,1,0:T(8,128)(2,1)S(1)}, u32[]{:S(2)}, u32[]{:S(2)}) collective-permute-start(bf16[2,144,512]{2,1,0:T(8,128)(2,1)S(1)} %collective-permute-done.3.refs_2_), channel_id=1, source_target_pairs={{2,3},{1,0},{6,7},{5,4},{10,11},{9,8},{14,15},{13,12},{18,19},{17,... | collective-permute-start | bytes 884744 | tf_op jit(solution)/shard_map/ppermute | solution.py:428
  21.9 13.6 %collective-permute-start.10 = (bf16[2,144,512]{2,1,0:T(8,128)(2,1)S(1)}, bf16[2,144,512]{2,1,0:T(8,128)(2,1)S(1)}, u32[]{:S(2)}, u32[]{:S(2)}) collective-permute-start(bf16[2,144,512]{2,1,0:T(8,128)(2,1)S(1)} %pad_maximum_fusion.3), channel_id=1, source_target_pairs={{4,8},{12,16},{20,24},{8,4},{16,12},{24,20},{5,9},{13,17},{21,25},... | collective-permute-start | bytes 884744 | tf_op jit(solution)/shard_map/ppermute | solution.py:421
  23.8 13.6 %collective-permute-start.4 = (bf16[2,144,512]{2,1,0:T(8,128)(2,1)S(1)}, bf16[2,144,512]{2,1,0:T(8,128)(2,1)S(1)}, u32[]{:S(2)}, u32[]{:S(2)}) collective-permute-start(bf16[2,144,512]{2,1,0:T(8,128)(2,1)S(1)} %pad_maximum_fusion.2), channel_id=1, source_target_pairs={{0,4},{4,0},{8,12},{12,8},{16,20},{20,16},{24,28},{28,24},{1,5},{5... | collective-permute-start | bytes 884744 | tf_op jit(solution)/shard_map/ppermute | solution.py:420
  31.0 22.5 %collective-permute-start.14 = (bf16[2,112,512]{2,1,0:T(8,128)(2,1)S(1)}, bf16[2,112,512]{2,1,0:T(8,128)(2,1)S(1)}, u32[]{:S(2)}, u32[]{:S(2)}) collective-permute-start(bf16[2,112,512]{2,1,0:T(8,128)(2,1)S(1)} %get-tuple-element.48.refs_0_), channel_id=1, source_target_pairs={{0,1},{1,0},{2,3},{3,2},{4,5},{5,4},{6,7},{7,6},{8,9},{9,8},{10,11... | collective-permute-start | bytes 688136 | tf_op jit(solution)/shard_map/ppermute | solution.py:433
  31.1 22.4 %collective-permute-start.15 = (bf16[2,112,512]{2,1,0:T(8,128)(2,1)S(1)}, bf16[2,112,512]{2,1,0:T(8,128)(2,1)S(1)}, u32[]{:S(2)}, u32[]{:S(2)}) collective-permute-start(bf16[2,112,512]{2,1,0:T(8,128)(2,1)S(1)} %get-tuple-element.48.refs_0_), channel_id=1, source_target_pairs={{0,2},{1,3},{2,0},{3,1},{4,6},{5,7},{6,4},{7,5},{8,10},{9,11},{10,... | collective-permute-start | bytes 688136 | tf_op jit(solution)/shard_map/ppermute | solution.py:433
  33.6 19.9 %collective-permute-start.16 = (bf16[2,112,512]{2,1,0:T(8,128)(2,1)S(1)}, bf16[2,112,512]{2,1,0:T(8,128)(2,1)S(1)}, u32[]{:S(2)}, u32[]{:S(2)}) collective-permute-start(bf16[2,112,512]{2,1,0:T(8,128)(2,1)S(1)} %get-tuple-element.48.refs_0_), channel_id=1, source_target_pairs={{0,3},{1,2},{2,1},{3,0},{4,7},{5,6},{6,5},{7,4},{8,11},{9,10},{10,... | collective-permute-start | bytes 688136 | tf_op jit(solution)/shard_map/ppermute | solution.py:433
  35.5 6.7 %collective-permute-start.11 = (bf16[1,144,512]{2,1,0:T(8,128)(2,1)S(1)}, bf16[1,144,512]{2,1,0:T(8,128)(2,1)S(1)}, u32[]{:S(2)}, u32[]{:S(2)}) collective-permute-start(bf16[1,144,512]{2,1,0:T(8,128)(2,1)S(1)} %get-tuple-element.53), channel_id=1, source_target_pairs={{4,8},{12,16},{20,24},{8,4},{16,12},{24,20},{5,9},{13,17},{21,25},... | collective-permute-start | bytes 442376 | tf_op jit(solution)/shard_map/ppermute | solution.py:421
  37.4 4.8 %collective-permute-start.9 = (bf16[1,144,512]{2,1,0:T(8,128)(2,1)S(1)}, bf16[1,144,512]{2,1,0:T(8,128)(2,1)S(1)}, u32[]{:S(2)}, u32[]{:S(2)}) collective-permute-start(bf16[1,144,512]{2,1,0:T(8,128)(2,1)S(1)} %get-tuple-element.54), channel_id=1, source_target_pairs={{0,4},{4,0},{8,12},{12,8},{16,20},{20,16},{24,28},{28,24},{1,5},{5... | collective-permute-start | bytes 442376 | tf_op jit(solution)/shard_map/ppermute | solution.py:420
  38.2 10.9 %slice-start = ((s8[6307840]{0:T(1024)(128)(4,1)}), s8[4194304]{0:T(1024)(128)(4,1)S(1)}, s32[]{:S(2)}) async-start(s8[6307840]{0:T(1024)(128)(4,1)} %bitcast.1), calls=%async_computation | async-start | bytes 8388608
  42.2 6.9 %slice-start.1 = ((s8[6307840]{0:T(1024)(128)(4,1)}), s8[2113536]{0:T(1024)(128)(4,1)S(1)}, s32[]{:S(2)}) async-start(s8[6307840]{0:T(1024)(128)(4,1)} %bitcast.1), calls=%async_computation.1 | async-start | bytes 4227072
  49.7 10.3 %collective-permute-start.12 = (bf16[1120,128]{1,0:T(8,128)(2,1)S(1)}, bf16[1120,128]{1,0:T(8,128)(2,1)S(1)}, u32[]{:S(2)}, u32[]{:S(2)}) collective-permute-start(bf16[1120,128]{1,0:T(8,128)(2,1)S(1)} %project_3.2), channel_id=1, source_target_pairs={{0,1},{3,2},{4,5},{7,6},{8,9},{11,10},{12,13},{15,14},{16,17},{19,... | collective-permute-start | bytes 860168 | tf_op jit(solution)/shard_map/ppermute | solution.py:524
  52.8 7.2 %collective-permute-start.13 = (bf16[1120,128]{1,0:T(8,128)(2,1)S(1)}, bf16[1120,128]{1,0:T(8,128)(2,1)S(1)}, u32[]{:S(2)}, u32[]{:S(2)}) collective-permute-start(bf16[1120,128]{1,0:T(8,128)(2,1)S(1)} %project_3.2), channel_id=1, source_target_pairs={{1,2},{2,1},{5,6},{6,5},{9,10},{10,9},{13,14},{14,13},{17,18},{18,... | collective-permute-start | bytes 860168 | tf_op jit(solution)/shard_map/ppermute | solution.py:525
  53.6 15.2 %collective-permute-start.18 = (bf16[3,112,512]{2,1,0:T(8,128)(2,1)S(1)}, bf16[3,112,512]{2,1,0:T(8,128)(2,1)S(1)}, u32[]{:S(2)}, u32[]{:S(2)}) collective-permute-start(bf16[3,112,512]{2,1,0:T(8,128)(2,1)S(1)} %pad_maximum_fusion.1), channel_id=1, source_target_pairs={{4,8},{12,16},{20,24},{8,4},{16,12},{24,20},{5,9},{13,17},{21,25},... | collective-permute-start | bytes 1032200 | tf_op jit(solution)/shard_map/ppermute | solution.py:421
  55.8 13.1 %collective-permute-start.17 = (bf16[3,112,512]{2,1,0:T(8,128)(2,1)S(1)}, bf16[3,112,512]{2,1,0:T(8,128)(2,1)S(1)}, u32[]{:S(2)}, u32[]{:S(2)}) collective-permute-start(bf16[3,112,512]{2,1,0:T(8,128)(2,1)S(1)} %pad_maximum_fusion), channel_id=1, source_target_pairs={{0,4},{4,0},{8,12},{12,8},{16,20},{20,16},{24,28},{28,24},{1,5},{5... | collective-permute-start | bytes 1032200 | tf_op jit(solution)/shard_map/ppermute | solution.py:420
  60.6 18.7 %collective-permute-start.20 = (bf16[1120,128]{1,0:T(8,128)(2,1)S(1)}, bf16[1120,128]{1,0:T(8,128)(2,1)S(1)}, u32[]{:S(2)}, u32[]{:S(2)}) collective-permute-start(bf16[1120,128]{1,0:T(8,128)(2,1)S(1)} %project_2.2), channel_id=1, source_target_pairs={{0,2},{1,3},{2,0},{3,1},{4,6},{5,7},{6,4},{7,5},{8,10},{9,11},{10,... | collective-permute-start | bytes 860168 | tf_op jit(solution)/shard_map/ppermute | solution.py:532
  68.8 12.6 %collective-permute-start.21 = (bf16[1120,128]{1,0:T(8,128)(2,1)S(1)}, bf16[1120,128]{1,0:T(8,128)(2,1)S(1)}, u32[]{:S(2)}, u32[]{:S(2)}) collective-permute-start(bf16[1120,128]{1,0:T(8,128)(2,1)S(1)} %project_1.2), channel_id=1, source_target_pairs={{0,1},{1,0},{2,3},{3,2},{4,5},{5,4},{6,7},{7,6},{8,9},{9,8},{10,11... | collective-permute-start | bytes 860168 | tf_op jit(solution)/shard_map/ppermute | solution.py:534
  74.7 6.7 %copy-start.5 = (s32[4]{0:T(128)S(1)}, s32[4]{0:T(128)}, u32[]{:S(2)}) copy-start(s32[4]{0:T(128)} %width_ref.7) | copy-start | bytes 52
  74.7 7.9 %collective-permute-start.19 = (bf16[848,128]{1,0:T(8,128)(2,1)S(1)}, bf16[848,128]{1,0:T(8,128)(2,1)S(1)}, u32[]{:S(2)}, u32[]{:S(2)}) collective-permute-start(bf16[848,128]{1,0:T(8,128)(2,1)S(1)} %project_3.3), channel_id=1, source_target_pairs={{0,1},{3,2},{4,5},{7,6},{8,9},{11,10},{12,13},{15,14},{16,17},{19,... | collective-permute-start | bytes 651272 | tf_op jit(solution)/shard_map/ppermute | solution.py:524
  78.7 8.5 %collective-permute-start.23 = (bf16[848,128]{1,0:T(8,128)(2,1)S(1)}, bf16[848,128]{1,0:T(8,128)(2,1)S(1)}, u32[]{:S(2)}, u32[]{:S(2)}) collective-permute-start(bf16[848,128]{1,0:T(8,128)(2,1)S(1)} %project_3.3), channel_id=1, source_target_pairs={{1,2},{2,1},{5,6},{6,5},{9,10},{10,9},{13,14},{14,13},{17,18},{18,... | collective-permute-start | bytes 651272 | tf_op jit(solution)/shard_map/ppermute | solution.py:525
  83.3 11.9 %collective-permute-start.22 = (bf16[848,128]{1,0:T(8,128)(2,1)S(1)}, bf16[848,128]{1,0:T(8,128)(2,1)S(1)}, u32[]{:S(2)}, u32[]{:S(2)}) collective-permute-start(bf16[848,128]{1,0:T(8,128)(2,1)S(1)} %project_2.3), channel_id=1, source_target_pairs={{0,2},{1,3},{2,0},{3,1},{4,6},{5,7},{6,4},{7,5},{8,10},{9,11},{10,... | collective-permute-start | bytes 651272 | tf_op jit(solution)/shard_map/ppermute | solution.py:532
  87.1 9.0 %collective-permute-start.24 = (bf16[848,128]{1,0:T(8,128)(2,1)S(1)}, bf16[848,128]{1,0:T(8,128)(2,1)S(1)}, u32[]{:S(2)}, u32[]{:S(2)}) collective-permute-start(bf16[848,128]{1,0:T(8,128)(2,1)S(1)} %project_1.3), channel_id=1, source_target_pairs={{0,1},{1,0},{2,3},{3,2},{4,5},{5,4},{6,7},{7,6},{8,9},{9,8},{10,11... | collective-permute-start | bytes 651272 | tf_op jit(solution)/shard_map/ppermute | solution.py:534
